TPU v7x, 256 devices: a whole 4x4x8 slice. The times are simulated.
256 devices in a mesh: tile: 64 (over x, z, y_lo), layer: 4 (over y_hi, core).
Axes of the slice: x: 4, y: 4 (y_hi: 2, y_lo: 2; y = y_hi * 2 + y_lo), z: 8, core: 2. Of those that a mesh axis runs over, the one named last changes fastest.
Arguments:
- velocity: float32 [2, 1024, 3072], P(None, 'tile'), may hold values from -6 to 6
- friction: float32 [1024, 3072], P('tile'), may hold values from -1 to 1
- thickness: float32 [1024, 3072], P('tile'), may hold values from 0.5 to 2
- rate: float32 [16, 1024, 3072], P('layer', 'tile'), may hold values from 0.5 to 2
- driving: float32 [2, 1024, 3072], P(None, 'tile'), may hold values from -6 to 6
- ice_mask: int32 [1024, 3072], P('tile'), may hold values from 0 to 2
- obs_velocity: float32 [64, 4, 64, 256], P('tile', 'layer'), may hold values from -6 to 6
- obs_weight: float32 [64, 4, 64, 128], P('tile', 'layer'), may hold values from 0.2 to 1
- obs_cells: int32 [64, 4, 64, 128], P('tile', 'layer'), may hold values from 0 to 49151
- obs_counts: int32 [64, 4, 64], P('tile', 'layer'), may hold values from 0 to 128, as said below
Outputs:
- friction_out: float32 [1024, 3072], P('tile')
- velocity_out: float32 [2, 1024, 3072], P(None, 'tile')
Inputs may be any that keep to these rules, and one draw needn't show every extreme that they name: `obs_counts`: in every draw one owner strip receives 128 live slots from every source share.
All inputs are finite; a program needn't handle non-finite values.
Results may differ from a plain program's by a relative error of at most 0.00002.
Values sent between devices are 32-bit elements; how exact they have to be, the bound alone decides.
A program may use at most 128 MiB of HBM per device.

v0:
```python
import jax
import jax.numpy as jnp
from jax import lax
from jax.sharding import PartitionSpec as P

ITERS = 2


def with_halo(block, sides, width):
    for axis, dim in sides:
        count = lax.axis_size(axis)
        forward = [(i, i + 1) for i in range(count - 1)]
        backward = [(target, source) for source, target in forward]
        low = lax.ppermute(
            lax.slice_in_dim(block, block.shape[dim] - width, None, axis=dim), axis, forward
        )
        high = lax.ppermute(lax.slice_in_dim(block, 0, width, axis=dim), axis, backward)
        block = jnp.concatenate([low, block, high], axis=dim)
    return block


def diff_rows(field):
    return 0.5 * (field[2:, :] - field[:-2, :])


def diff_cols(field):
    padded = jnp.pad(field, ((0, 0), (1, 1)))
    return 0.5 * (padded[:, 2:] - padded[:, :-2])


def layer_visc(exx, eyy, exy, speed, fric, thickness, rate):
    strain = exx * exx + eyy * eyy + exx * eyy + exy * exy + 0.05
    shear = 0.25 * fric * fric * (speed[0] * speed[0] + speed[1] * speed[1])
    depth_count = rate.shape[0]
    total_layers = depth_count * lax.axis_size("layer")
    first_layer = (lax.axis_index("layer") * depth_count).astype(jnp.float32)
    partial_sum = jnp.zeros_like(strain)
    for layer_k in range(depth_count):
        depth = 1.0 - (first_layer + layer_k + 0.5) / total_layers
        partial_sum = partial_sum + rate[layer_k] * (strain + depth * depth * shear) ** (-1.0 / 3.0)
    total = lax.psum(partial_sum, "layer")
    return thickness * (total / total_layers)


def body(
    velocity,
    friction,
    thickness,
    rate,
    driving,
    ice_mask,
    obs_velocity,
    obs_weight,
    obs_cells,
    obs_counts,
):
    grounded = (ice_mask == 2).astype(jnp.float32)
    icy = (ice_mask >= 1).astype(jnp.float32)
    slots = obs_weight.shape[-1]
    live = jnp.arange(slots, dtype=jnp.int32)[None, None, None, :] < obs_counts[..., None]
    weights = jnp.where(live, obs_weight, jnp.float32(0.0))
    packed = jnp.concatenate([obs_velocity, weights], axis=3)
    packed = lax.all_to_all(packed, "tile", split_axis=2, concat_axis=0, tiled=True)
    cells = lax.all_to_all(obs_cells, "tile", split_axis=2, concat_axis=0, tiled=True)
    columns = packed.reshape(-1, 3, slots)
    seen = jnp.stack([columns[:, 0, :].reshape(-1), columns[:, 1, :].reshape(-1)])
    slot_weight = columns[:, 2, :].reshape(-1)
    target = cells.reshape(-1)
    rows, width = friction.shape
    speed = velocity
    coeff = friction
    for step in range(ITERS):
        fric = grounded * jnp.exp(coeff)
        wide = with_halo(speed, (("tile", 1),), 1)
        exx = diff_rows(wide[0])
        eyy = diff_cols(speed[1])
        exy = 0.5 * (diff_cols(speed[0]) + diff_rows(wide[1]))
        visc = layer_visc(exx, eyy, exy, speed, fric, thickness, rate)
        sxx = 2.0 * visc * (2.0 * exx + eyy)
        syy = 2.0 * visc * (2.0 * eyy + exx)
        sxy = 2.0 * visc * exy
        stresses = jnp.stack([sxx, syy, sxy])
        rimmed = with_halo(stresses, (("tile", 1),), 1)
        div_a = diff_rows(rimmed[0]) + diff_cols(sxy)
        div_b = diff_rows(rimmed[2]) + diff_cols(syy)
        res_a = div_a - fric * speed[0] + driving[0]
        res_b = div_b - fric * speed[1] + driving[1]
        scale = 0.5 * icy / (1.0 + fric + 4.0 * visc)
        speed = jnp.stack([speed[0] + scale * res_a, speed[1] + scale * res_b])
        flat = speed.reshape(2, -1)
        picked = jnp.take(flat, target, axis=1)
        misfit = slot_weight[None, :] * (picked - seen)
        adjoint = jnp.zeros((2, rows * width), jnp.float32).at[:, target].add(misfit)
        adjoint = lax.psum(adjoint.reshape(2, rows, width), "layer")
        along = speed[0] * adjoint[0] + speed[1] * adjoint[1]
        coeff = coeff - 0.2 * fric * along
    return (coeff, speed)


def solution(mesh):
    placed = (
        P(None, "tile", None),
        P("tile", None),
        P("tile", None),
        P("layer", "tile", None),
        P(None, "tile", None),
        P("tile", None),
        P("tile", "layer", None, None),
        P("tile", "layer", None, None),
        P("tile", "layer", None, None),
        P("tile", "layer", None),
    )
    return jax.shard_map(
        body,
        mesh=mesh,
        in_specs=placed,
        out_specs=(P("tile", None), P(None, "tile", None)),
        check_vma=False,
    )
```

profile of v0, /device:TPU:1, one launch (start us, length us, event | category | flops | bytes accessed | tf_op | source)
XLA Modules:
  0.0 508.4 jit_solution(1730098218666725395)
XLA Ops:
  7.2 1.1 fusion.81
  8.2 4.0 collective-permute-start.1
  12.3 1.3 collective-permute-start
  13.6 14.6 %all-to-all-start = ((s32[1,1,64,128]{3,1,0,2:T(1,128)}), s32[1,1,64,128]{3,1,0,2:T(1,128)S(1)}, u32[]{:S(2)}, u32[]{:S(2)}) async-start(s32[1,1,64,128]{3,1,0,2:T(1,128)} %bitcast.205), calls=%async_computation | async-start | bytes 65536 | tf_op jit(solution)/shard_map/all_to_all | solution.py:64
  28.2 1.1 slice_bitcast_fusion.5
  29.2 1.0 constant_dynamic-update-slice_fusion
  30.3 0.8 fusion.74
  31.1 0.9 pad_maximum_fusion.20
  32.0 0.7 copy.42
  32.7 0.3 dynamic-update-slice.1
  33.0 3.6 fusion.64
  36.6 0.7 all-to-all-done
  37.3 10.0 %all-to-all-start.1 = ((f32[1,1,64,384]{3,1,0,2:T(1,128)}), f32[1,1,64,384]{3,1,0,2:T(1,128)S(1)}, u32[]{:S(2)}, u32[]{:S(2)}) async-start(f32[1,1,64,384]{3,1,0,2:T(1,128)} %copy.42), calls=%async_computation.1 | async-start | bytes 196608 | tf_op jit(solution)/shard_map/all_to_all | solution.py:63
  47.3 0.0 all-reduce.15.cloned.1.call-start
  47.5 9.3 %all-to-all-done.1 = f32[1,1,64,384]{3,1,0,2:T(1,128)S(1)} async-done(((f32[1,1,64,384]{3,1,0,2:T(1,128)}), f32[1,1,64,384]{3,1,0,2:T(1,128)S(1)}, u32[]{:S(2)}, u32[]{:S(2)}) %all-to-all-start.1) | async-done | bytes 98336 | tf_op jit(solution)/shard_map/all_to_all | solution.py:63
  56.8 0.2 reduce
  57.0 28.0 %all-reduce.13.cloned.1.call-done = f32[16,3072]{1,0:T(8,128)} async-done(((f32[16,3072]{1,0:T(8,128)}), f32[16,3072]{1,0:T(8,128)}) %all-reduce.13.cloned.1.call-update) | async-done | bytes 196624 | tf_op jit(solution)/shard_map/psum | solution.py:41
  85.1 1.2 multiply_bitcast_fusion.1
  86.3 0.2 multiply_multiply_fusion.5
  86.5 0.1 pad_maximum_fusion.27
  86.5 2.2 collective-permute-start.3
  88.8 1.3 collective-permute-start.2
  90.1 0.1 slice_bitcast_fusion.7
  90.1 4.0 collective-permute-done.2
  94.2 1.5 fusion.14
  95.6 1.3 fusion.21
  97.0 0.2 copy.52
  97.2 0.2 copy.51
  97.4 0.4 pad_maximum_fusion
  97.7 12.3 %copy.43 = f32[2,49152]{0,1:T(8,128)} copy(f32[2,49152]{1,0:T(2,128)S(1)} %pad_maximum_fusion) | data formatting | bytes 786432 | tf_op jit(solution)/shard_map/stack | solution.py:89
  110.0 36.1 %gather_fusion = f32[8192,2]{1,0:T(8,128)} fusion(f32[2,49152]{0,1:T(8,128)} %copy.43, s32[8192]{0:T(1024)S(1)} %fusion.75), kind=kCustom, calls=%fused_computation.clone | custom fusion | bytes 163840 | tf_op jit(solution)/shard_map/jit(_take)/gather | solution.py:91
  146.1 2.8 copy.44
  148.9 0.1 fusion.73
  149.0 2.7 copy.45
  151.7 54.2 %scatter_custom_fusion = f32[2,49152]{0,1:T(8,128)} fusion(s32[8192]{0:T(1024)S(1)} %bitcast.206, f32[8192,2]{1,0:T(8,128)} %copy.45, f32[]{:T(128)} %constant.28.clone.1), kind=kCustom, calls=%fused_computation.6 | custom fusion | flops 16384 | bytes 393728 | tf_op jit(solution)/shard_map/scatter-add | solution.py:93
  205.9 14.5 %copy.46 = f32[2,16,3072]{2,1,0:T(8,128)} copy(f32[2,16,3072]{0,2,1:T(8,128)} %bitcast.174) | data formatting | bytes 786432 | tf_op jit(solution)/shard_map/reshape | solution.py:94
  220.4 0.0 all-reduce.17.cloned.1.call-start
  220.5 4.3 collective-permute-start.5
  224.8 1.3 collective-permute-start.4
  226.1 3.3 collective-permute-done.4
  229.4 40.3 %all-reduce.15.cloned.1.call-done = f32[2,16,3072]{2,1,0:T(8,128)} async-done(((f32[2,16,3072]{2,1,0:T(8,128)}), f32[2,16,3072]{2,1,0:T(8,128)}) %all-reduce.15.cloned.1.call-update) | async-done | bytes 393232 | tf_op jit(solution)/shard_map/psum | solution.py:94
  269.7 3.1 fusion.65
  272.8 45.1 %all-reduce.17.cloned.1.call-done = f32[16,3072]{1,0:T(8,128)} async-done(((f32[16,3072]{1,0:T(8,128)}), f32[16,3072]{1,0:T(8,128)}) %all-reduce.17.cloned.1.call-update) | async-done | bytes 196624 | tf_op jit(solution)/shard_map/psum | solution.py:41
  318.0 1.1 multiply_bitcast_fusion
  319.1 0.2 multiply_multiply_fusion.4
  319.3 0.1 pad_maximum_fusion.24
  319.3 2.2 collective-permute-start.7
  321.6 1.3 collective-permute-start.6
  322.9 4.1 collective-permute-done.6
  327.0 0.2 fusion.39
  327.2 0.2 copy.54
  327.4 0.2 fusion.32
  327.6 0.2 copy.53
  327.8 0.4 pad_maximum_fusion.1
  328.2 12.3 %copy.47 = f32[2,49152]{0,1:T(8,128)} copy(f32[2,49152]{1,0:T(2,128)S(1)} %pad_maximum_fusion.1) | data formatting | bytes 786432 | tf_op jit(solution)/shard_map/stack | solution.py:89
  340.4 36.1 %gather_fusion.1 = f32[8192,2]{1,0:T(8,128)} fusion(f32[2,49152]{0,1:T(8,128)} %copy.47, s32[8192]{0:T(1024)S(1)} %fusion.75), kind=kCustom, calls=%fused_computation.1.clone | custom fusion | bytes 163840 | tf_op jit(solution)/shard_map/jit(_take)/gather | solution.py:91
  376.5 2.8 copy.48
  379.4 0.1 fusion.71
  379.5 2.7 copy.49
  382.1 54.2 %scatter_custom_fusion.1 = f32[2,49152]{0,1:T(8,128)} fusion(s32[8192]{0:T(1024)S(1)} %bitcast.207, f32[8192,2]{1,0:T(8,128)} %copy.49, f32[]{:T(128)} %constant.28.clone.1), kind=kCustom, calls=%fused_computation.4 | custom fusion | flops 16384 | bytes 393728 | tf_op jit(solution)/shard_map/scatter-add | solution.py:93
  436.3 14.5 %copy.50 = f32[2,16,3072]{2,1,0:T(8,128)} copy(f32[2,16,3072]{0,2,1:T(8,128)} %bitcast.173) | data formatting | bytes 786432 | tf_op jit(solution)/shard_map/reshape | solution.py:94
  450.9 0.8 pad_maximum_fusion.2
  451.6 48.5 %all-reduce.19.cloned.1.call-done = f32[2,16,3072]{2,1,0:T(8,128)} async-done(((f32[2,16,3072]{2,1,0:T(8,128)}), f32[2,16,3072]{2,1,0:T(8,128)}) %all-reduce.19.cloned.1.call-update) | async-done | bytes 393232 | tf_op jit(solution)/shard_map/psum | solution.py:94
  500.1 1.8 fusion.45
  (24 shorter events, 0.3 us)
Async XLA Ops:
  8.2 24.8 %collective-permute-start.1 = (f32[2,1,3072]{2,1,0:T(1,128)S(1)}, f32[2,1,3072]{2,1,0:T(1,128)S(1)}, u32[]{:S(2)}, u32[]{:S(2)}) collective-permute-start(f32[2,1,3072]{2,1,0:T(1,128)S(1)} %get-tuple-element.26), channel_id=1, source_target_pairs={{0,4},{4,8},{8,12},{12,16},{16,20},{20,24},{24,28},{28,32},{32,36}... | collective-permute-start | bytes 73736 | tf_op jit(solution)/shard_map/ppermute | solution.py:14
  12.3 20.4 %collective-permute-start = (f32[2,1,3072]{2,1,0:T(1,128)S(1)}, f32[2,1,3072]{2,1,0:T(1,128)S(1)}, u32[]{:S(2)}, u32[]{:S(2)}) collective-permute-start(f32[2,1,3072]{2,1,0:T(1,128)S(1)} %get-tuple-element.25), channel_id=1, source_target_pairs={{4,0},{8,4},{12,8},{16,12},{20,16},{24,20},{28,24},{32,28},{36,32}... | collective-permute-start | bytes 73736 | tf_op jit(solution)/shard_map/ppermute | solution.py:17
  13.6 23.7 %all-to-all-start = ((s32[1,1,64,128]{3,1,0,2:T(1,128)}), s32[1,1,64,128]{3,1,0,2:T(1,128)S(1)}, u32[]{:S(2)}, u32[]{:S(2)}) async-start(s32[1,1,64,128]{3,1,0,2:T(1,128)} %bitcast.205), calls=%async_computation | async-start | bytes 65536 | tf_op jit(solution)/shard_map/all_to_all | solution.py:64
  28.1 57.0 %all-reduce.13.cloned.1.call-start = ((), (), s32[]{:S(2)}) async-start(), calls=%async_computation.2 | async-start | bytes 393216 | tf_op jit(solution)/shard_map/psum | solution.py:41
  37.3 19.5 %all-to-all-start.1 = ((f32[1,1,64,384]{3,1,0,2:T(1,128)}), f32[1,1,64,384]{3,1,0,2:T(1,128)S(1)}, u32[]{:S(2)}, u32[]{:S(2)}) async-start(f32[1,1,64,384]{3,1,0,2:T(1,128)} %copy.42), calls=%async_computation.1 | async-start | bytes 196608 | tf_op jit(solution)/shard_map/all_to_all | solution.py:63
  47.3 222.4 %all-reduce.15.cloned.1.call-start = ((), (), s32[]{:S(2)}) async-start(), calls=%async_computation.3 | async-start | bytes 786432 | tf_op jit(solution)/shard_map/psum | solution.py:94
  86.5 3.6 collective-permute-start.3
  88.8 5.4 %collective-permute-start.2 = (f32[3,1,3072]{2,1,0:T(1,128)S(1)}, f32[3,1,3072]{2,1,0:T(1,128)S(1)}, u32[]{:S(2)}, u32[]{:S(2)}) collective-permute-start(f32[3,1,3072]{2,1,0:T(1,128)S(1)} %get-tuple-element.19), channel_id=1, source_target_pairs={{4,0},{8,4},{12,8},{16,12},{20,16},{24,20},{28,24},{32,28},{36,32}... | collective-permute-start | bytes 110600 | tf_op jit(solution)/shard_map/ppermute | solution.py:17
  151.7 118.0 %copy-start = (f32[16,3072]{1,0:T(8,128)S(1)}, f32[16,3072]{1,0:T(8,128)}, u32[]{:S(2)}) copy-start(f32[16,3072]{1,0:T(8,128)} %param.13) | copy-start | bytes 589828
  151.7 118.0 %copy-start.1 = (f32[4,16,3072]{2,1,0:T(8,128)S(1)}, f32[4,16,3072]{2,1,0:T(8,128)}, u32[]{:S(2)}) copy-start(f32[4,16,3072]{2,1,0:T(8,128)} %param.15) | copy-start | bytes 2359300
  151.7 166.3 %copy-start.3 = (f32[16,3072]{1,0:T(8,128)S(1)}, f32[16,3072]{1,0:T(8,128)}, u32[]{:S(2)}) copy-start(f32[16,3072]{1,0:T(8,128)} %param.14) | copy-start | bytes 589828
  151.7 175.2 %copy-start.2 = (f32[2,16,3072]{2,1,0:T(8,128)S(1)}, f32[2,16,3072]{2,1,0:T(8,128)}, u32[]{:S(2)}) copy-start(f32[2,16,3072]{2,1,0:T(8,128)} %param.16) | copy-start | bytes 1179652
  220.4 97.5 %all-reduce.17.cloned.1.call-start = ((), (), s32[]{:S(2)}) async-start(), calls=%async_computation.4 | async-start | bytes 393216 | tf_op jit(solution)/shard_map/psum | solution.py:41
  220.5 5.6 %collective-permute-start.5 = (f32[2,1,3072]{2,1,0:T(1,128)S(1)}, f32[2,1,3072]{2,1,0:T(1,128)S(1)}, u32[]{:S(2)}, u32[]{:S(2)}) collective-permute-start(f32[2,1,3072]{2,1,0:T(1,128)S(1)} %get-tuple-element.22), channel_id=1, source_target_pairs={{0,4},{4,8},{8,12},{12,16},{16,20},{20,24},{24,28},{28,32},{32,36}... | collective-permute-start | bytes 73736 | tf_op jit(solution)/shard_map/ppermute | solution.py:14
  224.8 4.6 collective-permute-start.4
  272.8 227.3 %all-reduce.19.cloned.1.call-start = ((), (), s32[]{:S(2)}) async-start(), calls=%async_computation.5 | async-start | bytes 786432 | tf_op jit(solution)/shard_map/psum | solution.py:94
  319.3 3.5 collective-permute-start.7
  321.6 5.4 %collective-permute-start.6 = (f32[3,1,3072]{2,1,0:T(1,128)S(1)}, f32[3,1,3072]{2,1,0:T(1,128)S(1)}, u32[]{:S(2)}, u32[]{:S(2)}) collective-permute-start(f32[3,1,3072]{2,1,0:T(1,128)S(1)} %get-tuple-element.17), channel_id=1, source_target_pairs={{4,0},{8,4},{12,8},{16,12},{20,16},{24,20},{28,24},{32,28},{36,32}... | collective-permute-start | bytes 110600 | tf_op jit(solution)/shard_map/ppermute | solution.py:17
Sparse Core Ops, SparseCore 0:
  36.7 48.3 all-reduce.12
  220.6 49.0 all-reduce.14
  272.9 45.0 all-reduce.16
  451.0 49.0 all-reduce.18
where the time goes:
time: 510 us; the launch traced here: 508 us
  waiting for transfers between devices  183 us (36%)
  local copies, waits for them, and re-layouts  142 us (28%)
  other arithmetic  127 us (25%)
  starting transfers between devices  42.7 us (8%)
  between operations  14 us (3%)
    scatter-add x2, other arithmetic, body(): jnp.zeros((2, rows * width), jnp.float32).at[:, target].add(misfit)  108 us
    psum x2, waiting for transfers between devices, body(): adjoint = lax.psum(adjoint.reshape(2, rows, width), 'layer')  88.7 us
    gather x4, local copies, waits for them, and re-layouts, body(): picked = jnp.take(flat, target, axis=1)  77.8 us
    psum x2, waiting for transfers between devices, layer_visc(): total = lax.psum(partial_sum, 'layer')  73.2 us
    reshape x2, local copies, waits for them, and re-layouts, body(): adjoint = lax.psum(adjoint.reshape(2, rows, width), 'layer')  29 us
    another operation x2, local copies, waits for them, and re-layouts, body(): speed = jnp.stack([speed[0] + scale * res_a, speed[1] + scale * res_b])  24.5 us
    all_to_all x1, starting transfers between devices, body(): lax.all_to_all(obs_cells, 'tile', split_axis=2, concat_axis=0, tiled=True)  14.6 us
    ppermute x4, starting transfers between devices, with_halo(): lax.ppermute(lax.slice_in_dim(block, block.shape[dim] - width, None, axis...  12.7 us
  transfers between devices with their start and end apart: 14, of which 9 were waited for; matrix products, arithmetic and copies ran while one was open for 2% of the time, Pallas kernels for 0%

commit v1 on v0

v1 whole, which is shorter than its diff:
```python
import functools
import math

import jax
import jax.numpy as jnp
from jax import lax
from jax.experimental import pallas as pl
from jax.experimental.pallas import tpu as pltpu
from jax.sharding import PartitionSpec as P

ITERS = 2
MESH = pl.DeviceIdType.MESH
LANES = 128
PIECES = 3
CHANNELS = 3


def split_pieces(value):
    pieces = []
    for _ in range(PIECES):
        piece = value.astype(jnp.bfloat16).astype(jnp.float32)
        pieces.append(piece)
        value = value - piece
    return pieces


def kernel(
    n_tile,
    n_layer,
    groups,
    velocity,
    friction,
    thickness,
    rate,
    driving,
    ice_mask,
    obs_velocity,
    obs_weight,
    obs_cells,
    obs_counts,
    friction_out,
    velocity_out,
    packed,
    received,
    left_side,
    right_side,
    total,
    fields,
    from_sibling,
    pair_sum,
    from_partner,
    rates,
    vel,
    edge_left,
    edge_right,
    fric_in,
    thick,
    drive,
    mask,
    row_send,
    row_recv,
    col_send,
    col_recv,
    result,
    load_sems,
    obs_send_sem,
    obs_recv_sems,
    rate_send_sems,
    rate_recv_sems,
    row_send_sems,
    row_recv_sems,
    col_send_sems,
    col_recv_sems,
    sum_send_sems,
    sum_recv_sems,
    out_send_sems,
    out_recv_sems,
    own_sems,
):
    t = lax.axis_index("tile")
    l = lax.axis_index("layer")
    rows, width = friction.shape
    quarter = width // n_layer
    depth = rate.shape[0]
    total_layers = depth * n_layer
    slots = obs_weight.shape[-1]
    per_group = n_tile // groups
    marks = rows * n_layer
    core = lax.rem(l, 2)
    pair = l // 2
    sibling = pair * 2 + (1 - core)
    partner = (1 - pair) * 2 + core
    above = lax.rem(t + n_tile - 1, n_tile)
    below = lax.rem(t + 1, n_tile)
    lefter = lax.rem(l + n_layer - 1, n_layer)
    righter = lax.rem(l + 1, n_layer)
    first = pl.multiple_of(l * quarter, LANES)
    columns = pl.ds(first, quarter)

    def remote(src, dst, send_sem, recv_sem, tile, layer):
        return pltpu.make_async_remote_copy(
            src_ref=src,
            dst_ref=dst,
            send_sem=send_sem,
            recv_sem=recv_sem,
            device_id=(tile, layer),
            device_id_type=MESH,
        )

    before = pl.multiple_of(jnp.maximum(first - LANES, 0), LANES)
    after = pl.multiple_of(jnp.minimum(first + quarter, width - LANES), LANES)
    loads = [
        pltpu.make_async_copy(velocity.at[:, :, columns], vel, load_sems.at[0]),
        pltpu.make_async_copy(velocity.at[:, :, pl.ds(before, LANES)], edge_left, load_sems.at[1]),
        pltpu.make_async_copy(velocity.at[:, :, pl.ds(after, LANES)], edge_right, load_sems.at[2]),
        pltpu.make_async_copy(friction.at[:, columns], fric_in, load_sems.at[3]),
        pltpu.make_async_copy(thickness.at[:, columns], thick, load_sems.at[4]),
        pltpu.make_async_copy(driving.at[:, :, columns], drive, load_sems.at[5]),
        pltpu.make_async_copy(ice_mask.at[:, columns], mask, load_sems.at[6]),
        pltpu.make_async_copy(
            rate.at[:, :, columns], rates.at[pl.ds(l * depth, depth)], load_sems.at[7]
        ),
    ]
    for load in loads:
        load.start()

    barrier = pltpu.get_barrier_semaphore()

    def greet(offset, carry):
        pl.semaphore_signal(
            barrier, inc=1, device_id=(lax.rem(t + offset, n_tile), l), device_id_type=MESH
        )
        return carry

    lax.fori_loop(1, n_tile, greet, 0)
    for offset in range(1, n_layer):
        pl.semaphore_signal(
            barrier, inc=1, device_id=(t, lax.rem(l + offset, n_layer)), device_id_type=MESH
        )

    row_id = lax.broadcasted_iota(jnp.int32, (n_tile, n_tile), 0)
    col_id = lax.broadcasted_iota(jnp.int32, (n_tile, n_tile), 1)
    counts = jnp.sum(
        jnp.where(row_id == col_id, obs_counts[...].astype(jnp.float32), 0.0), axis=1, keepdims=True
    )
    place = lax.broadcasted_iota(jnp.int32, (n_tile, slots), 1).astype(jnp.float32)
    weight = jnp.where(place < counts, obs_weight[...], 0.0)
    packed[:, 0, :] = weight
    packed[:, 1, :] = weight * obs_velocity[:, :slots]
    packed[:, 2, :] = weight * obs_velocity[:, slots:]
    packed[:, 3, :] = obs_cells[...].astype(jnp.float32)
    received[0] = packed[t]

    for load in loads[:3]:
        load.wait()
    row_send[0, 0] = vel[:, 0, :]
    row_send[0, 1] = vel[:, rows - 1, :]

    pl.semaphore_wait(barrier, n_tile - 1 + n_layer - 1)

    def swap_rows(phase):
        copies = [
            remote(
                row_send.at[phase, 0],
                row_recv.at[phase, 1],
                row_send_sems.at[phase, 0],
                row_recv_sems.at[phase, 1],
                above,
                l,
            ),
            remote(
                row_send.at[phase, 1],
                row_recv.at[phase, 0],
                row_send_sems.at[phase, 1],
                row_recv_sems.at[phase, 0],
                below,
                l,
            ),
        ]
        for copy in copies:
            copy.start()
        return copies

    def swap_cols(phase):
        copies = [
            remote(
                col_send.at[phase, 0],
                col_recv.at[phase, 1],
                col_send_sems.at[phase, 0],
                col_recv_sems.at[phase, 1],
                t,
                lefter,
            ),
            remote(
                col_send.at[phase, 1],
                col_recv.at[phase, 0],
                col_send_sems.at[phase, 1],
                col_recv_sems.at[phase, 0],
                t,
                righter,
            ),
        ]
        for copy in copies:
            copy.start()
        return copies

    def send_edges(phase, by_row, by_col):
        for k in range(2):
            row_send[phase, 0, k : k + 1, :] = by_row[k][0:1, :]
            row_send[phase, 1, k : k + 1, :] = by_row[k][rows - 1 : rows, :]
            col_send[phase - 1, 0, k] = by_col[k][:, :LANES]
            col_send[phase - 1, 1, k] = by_col[k][:, quarter - LANES :]
        return swap_rows(phase) + swap_cols(phase - 1)

    first_rows = swap_rows(0)

    def send_obs(offset, carry):
        to = lax.rem(t + offset, n_tile)
        remote(
            packed.at[to],
            received.at[offset],
            obs_send_sem,
            obs_recv_sems.at[offset // per_group],
            to,
            l,
        ).start()
        return carry

    lax.fori_loop(1, n_tile, send_obs, 0)

    rate_copies = []
    for offset in (1, 2, 3):
        to = lax.rem(l + offset, n_layer)
        copy = remote(
            rate.at[:, :, pl.ds(pl.multiple_of(to * quarter, LANES), quarter)],
            rates.at[pl.ds(l * depth, depth)],
            rate_send_sems.at[offset - 1],
            rate_recv_sems.at[offset - 1],
            t,
            to,
        )
        copy.start()
        rate_copies.append(copy)

    total[...] = jnp.zeros_like(total)
    mark_id = lax.broadcasted_iota(jnp.int32, (marks, slots), 0).astype(jnp.float32)
    lane_id = lax.broadcasted_iota(jnp.int32, (slots, quarter), 1).astype(jnp.float32)

    def gather_group(group, count, start):
        return pltpu.make_async_copy(
            received.at[pl.ds(start, count)], received.at[pl.ds(start, count)], obs_recv_sems.at[group]
        )

    def add_group(group):
        block = received[pl.ds(group * per_group, per_group)]
        cell = block[:, 3, :]
        mark = jnp.floor((cell + 0.5) * (1.0 / quarter))
        column = cell - mark * quarter
        row = jnp.floor((mark + 0.5) * (1.0 / n_layer))
        mark = (mark - row * n_layer) * rows + row
        column = column.T
        pieces = []
        for channel in range(CHANNELS):
            pieces += split_pieces(block[:, channel, :])
        for b in range(per_group):
            hit = mark[b : b + 1, :] == mark_id
            for p, piece in enumerate(pieces):
                left_side[p * marks : (p + 1) * marks, b * slots : (b + 1) * slots] = jnp.where(
                    hit, piece[b : b + 1, :], 0.0
                ).astype(jnp.bfloat16)
            right_side[b * slots : (b + 1) * slots, :] = jnp.where(
                column[:, b : b + 1] == lane_id, 1.0, 0.0
            ).astype(jnp.bfloat16)
        total[...] += jnp.dot(left_side[...], right_side[...], preferred_element_type=jnp.float32)

    gather_group(0, per_group - 1, 1).wait()
    add_group(0)

    def later_group(group, carry):
        gather_group(group, per_group, group * per_group).wait()
        add_group(group)
        return carry

    lax.fori_loop(1, groups, later_group, 0)

    def collect(q):
        for channel in range(CHANNELS):
            field = None
            for piece in range(PIECES):
                start = pl.multiple_of((channel * PIECES + piece) * marks + q * rows, rows)
                part = total[pl.ds(start, rows), :]
                field = part if field is None else field + part
            fields[q, channel] = field

    sum_copies = []
    for k, chip in enumerate((1 - pair, pair)):
        q = chip * 2 + (1 - core)
        collect(q)
        copy = remote(
            fields.at[q], from_sibling.at[k], sum_send_sems.at[k], sum_recv_sems.at[k], t, sibling
        )
        copy.start()
        sum_copies.append(copy)
    collect(partner)

    for load in loads[3:]:
        load.wait()
    for copy in rate_copies:
        copy.wait()
    for copy in first_rows:
        copy.wait()

    row_of = lax.broadcasted_iota(jnp.int32, (rows, quarter), 0)
    col_of = lax.broadcasted_iota(jnp.int32, (rows, quarter), 1)
    top, bottom = t == 0, t == n_tile - 1
    leftmost, rightmost = l == 0, l == n_layer - 1

    def diff_rows(field, low, high):
        low = jnp.where(top, 0.0, low)
        high = jnp.where(bottom, 0.0, high)
        previous = jnp.where(row_of == 0, low, pltpu.roll(field, 1, 0))
        following = jnp.where(row_of == rows - 1, high, pltpu.roll(field, rows - 1, 0))
        return 0.5 * (following - previous)

    def diff_cols(field, low, high):
        low = jnp.where(leftmost, 0.0, low)
        high = jnp.where(rightmost, 0.0, high)
        previous = jnp.where(col_of == 0, low, pltpu.roll(field, 1, 1))
        following = jnp.where(col_of == quarter - 1, high, pltpu.roll(field, quarter - 1, 1))
        return 0.5 * (following - previous)

    def row_halo(phase, k):
        return row_recv[phase, 0, k : k + 1, :], row_recv[phase, 1, k : k + 1, :]

    def col_halo(phase, k):
        return (
            col_recv[phase - 1, 0, k, :, LANES - 1 : LANES],
            col_recv[phase - 1, 1, k, :, 0:1],
        )

    grounded = jnp.where(mask[...] == 2, 1.0, 0.0)
    icy = jnp.where(mask[...] >= 1, 1.0, 0.0)

    def strains(speed, rows_0, rows_1, cols_0, cols_1):
        exx = diff_rows(speed[0], *rows_0)
        eyy = diff_cols(speed[1], *cols_1)
        exy = 0.5 * (diff_cols(speed[0], *cols_0) + diff_rows(speed[1], *rows_1))
        return exx, eyy, exy

    def viscosity(strain, speed, fric):
        exx, eyy, exy = strain
        e2 = exx * exx + eyy * eyy + exx * eyy + exy * exy + 0.05
        b2 = 0.25 * fric * fric * (speed[0] * speed[0] + speed[1] * speed[1])
        total_visc = jnp.zeros_like(e2)
        for k in range(total_layers):
            height = 1.0 - (k + 0.5) / total_layers
            total_visc = total_visc + rates[k] * jnp.exp(
                jnp.log(e2 + (height * height) * b2) * (-1.0 / 3.0)
            )
        return thick[...] * (total_visc * (1.0 / total_layers))

    def stresses(strain, visc):
        exx, eyy, exy = strain
        return 2.0 * visc * (2.0 * exx + eyy), 2.0 * visc * (2.0 * eyy + exx), 2.0 * visc * exy

    def new_speed(speed, fric, visc, stress, phase):
        sxx, syy, sxy = stress
        div_0 = diff_rows(sxx, *row_halo(phase, 0)) + diff_cols(sxy, *col_halo(phase, 0))
        div_1 = diff_rows(sxy, *row_halo(phase, 1)) + diff_cols(syy, *col_halo(phase, 1))
        scale = 0.5 * icy / (1.0 + fric + 4.0 * visc)
        return (
            speed[0] + scale * (div_0 - fric * speed[0] + drive[0]),
            speed[1] + scale * (div_1 - fric * speed[1] + drive[1]),
        )

    speed = (vel[0], vel[1])
    coeff = fric_in[...]
    fric = grounded * jnp.exp(coeff)
    strain = strains(
        speed,
        row_halo(0, 0),
        row_halo(0, 1),
        (edge_left[0, :, LANES - 1 : LANES], edge_right[0, :, 0:1]),
        (edge_left[1, :, LANES - 1 : LANES], edge_right[1, :, 0:1]),
    )
    visc = viscosity(strain, speed, fric)
    stress = stresses(strain, visc)
    edges = send_edges(1, (stress[0], stress[2]), (stress[2], stress[1]))

    sum_copies[0].wait()
    pair_sum[...] = fields[partner] + from_sibling[0]
    cross = remote(pair_sum, from_partner, sum_send_sems.at[2], sum_recv_sems.at[2], t, partner)
    cross.start()
    collect(l)

    for copy in edges:
        copy.wait()
    speed = new_speed(speed, fric, visc, stress, 1)
    edges = send_edges(2, speed, speed)
    sum_copies[1].wait()
    for channel in range(CHANNELS):
        fields[l, channel] = fields[l, channel] + from_sibling[1, channel]
    for copy in edges:
        copy.wait()
    strain = strains(speed, row_halo(2, 0), row_halo(2, 1), col_halo(2, 0), col_halo(2, 1))
    cross.wait()
    weight_sum, seen_0, seen_1 = (fields[l, k] + from_partner[k] for k in range(CHANNELS))

    def new_coeff(coeff, fric, speed):
        along = speed[0] * (weight_sum * speed[0] - seen_0) + speed[1] * (
            weight_sum * speed[1] - seen_1
        )
        return coeff - 0.2 * fric * along

    coeff = new_coeff(coeff, fric, speed)

    fric = grounded * jnp.exp(coeff)
    visc = viscosity(strain, speed, fric)
    stress = stresses(strain, visc)
    for copy in send_edges(3, (stress[0], stress[2]), (stress[2], stress[1])):
        copy.wait()
    speed = new_speed(speed, fric, visc, stress, 3)
    result[0] = speed[0]
    result[1] = speed[1]
    result[2] = new_coeff(coeff, fric, speed)

    finals = [
        pltpu.make_async_copy(result.at[0:2], velocity_out.at[:, :, columns], own_sems.at[0]),
        pltpu.make_async_copy(result.at[2], friction_out.at[:, columns], own_sems.at[1]),
    ]
    for copy in finals:
        copy.start()
    for offset in (1, 2, 3):
        to = lax.rem(l + offset, n_layer)
        pairs = (
            (result.at[0:2], velocity_out.at[:, :, columns]),
            (result.at[2], friction_out.at[:, columns]),
        )
        for k, (src, dst) in enumerate(pairs):
            copy = remote(
                src, dst, out_send_sems.at[offset - 1, k], out_recv_sems.at[offset - 1, k], t, to
            )
            copy.start()
            finals.append(copy)
    for copy in finals:
        copy.wait()

    pltpu.make_async_copy(
        packed.at[pl.ds(1, n_tile - 1)], packed.at[pl.ds(1, n_tile - 1)], obs_send_sem
    ).wait()


def body(
    velocity,
    friction,
    thickness,
    rate,
    driving,
    ice_mask,
    obs_velocity,
    obs_weight,
    obs_cells,
    obs_counts,
):
    n_tile, n_layer = lax.axis_size("tile"), lax.axis_size("layer")
    rows, width = friction.shape
    quarter = width // n_layer
    slots = obs_weight.shape[-1]
    depth = rate.shape[0]
    groups = 8 if n_tile % 8 == 0 else 2
    marks = rows * n_layer
    chunk = (n_tile // groups) * slots
    anywhere = pl.BlockSpec(memory_space=pl.ANY)
    in_vmem = pl.BlockSpec(memory_space=pltpu.VMEM)
    f32 = jnp.float32
    friction_out, velocity_out = pl.pallas_call(
        functools.partial(kernel, n_tile, n_layer, groups),
        out_shape=(
            jax.ShapeDtypeStruct(friction.shape, f32),
            jax.ShapeDtypeStruct(velocity.shape, f32),
        ),
        in_specs=[anywhere] * 6 + [in_vmem] * 4,
        out_specs=(anywhere, anywhere),
        scratch_shapes=[
            pltpu.VMEM((n_tile, 4, slots), f32),
            pltpu.VMEM((n_tile, 4, slots), f32),
            pltpu.VMEM((CHANNELS * PIECES * marks, chunk), jnp.bfloat16),
            pltpu.VMEM((chunk, quarter), jnp.bfloat16),
            pltpu.VMEM((CHANNELS * PIECES * marks, quarter), f32),
            pltpu.VMEM((n_layer, CHANNELS, rows, quarter), f32),
            pltpu.VMEM((2, CHANNELS, rows, quarter), f32),
            pltpu.VMEM((CHANNELS, rows, quarter), f32),
            pltpu.VMEM((CHANNELS, rows, quarter), f32),
            pltpu.VMEM((depth * n_layer, rows, quarter), f32),
            pltpu.VMEM((2, rows, quarter), f32),
            pltpu.VMEM((2, rows, LANES), f32),
            pltpu.VMEM((2, rows, LANES), f32),
            pltpu.VMEM((rows, quarter), f32),
            pltpu.VMEM((rows, quarter), f32),
            pltpu.VMEM((2, rows, quarter), f32),
            pltpu.VMEM((rows, quarter), jnp.int32),
            pltpu.VMEM((4, 2, 2, quarter), f32),
            pltpu.VMEM((4, 2, 2, quarter), f32),
            pltpu.VMEM((3, 2, 2, rows, LANES), f32),
            pltpu.VMEM((3, 2, 2, rows, LANES), f32),
            pltpu.VMEM((3, rows, quarter), f32),
            pltpu.SemaphoreType.DMA((8,)),
            pltpu.SemaphoreType.DMA,
            pltpu.SemaphoreType.DMA((groups,)),
            pltpu.SemaphoreType.DMA((3,)),
            pltpu.SemaphoreType.DMA((3,)),
            pltpu.SemaphoreType.DMA((4, 2)),
            pltpu.SemaphoreType.DMA((4, 2)),
            pltpu.SemaphoreType.DMA((3, 2)),
            pltpu.SemaphoreType.DMA((3, 2)),
            pltpu.SemaphoreType.DMA((3,)),
            pltpu.SemaphoreType.DMA((3,)),
            pltpu.SemaphoreType.DMA((3, 2)),
            pltpu.SemaphoreType.DMA((3, 2)),
            pltpu.SemaphoreType.DMA((2,)),
        ],
        compiler_params=pltpu.CompilerParams(
            collective_id=0, has_side_effects=True, vmem_limit_bytes=40 * 1024 * 1024
        ),
    )(
        velocity,
        friction,
        thickness,
        rate,
        driving,
        ice_mask,
        obs_velocity.reshape(n_tile, 2 * slots),
        obs_weight.reshape(n_tile, slots),
        obs_cells.reshape(n_tile, slots),
        obs_counts.reshape(1, n_tile),
    )
    return friction_out, velocity_out


def solution(mesh):
    placed = (
        P(None, "tile", None),
        P("tile", None),
        P("tile", None),
        P("layer", "tile", None),
        P(None, "tile", None),
        P("tile", None),
        P("tile", "layer", None, None),
        P("tile", "layer", None, None),
        P("tile", "layer", None, None),
        P("tile", "layer", None),
    )
    return jax.shard_map(
        body,
        mesh=mesh,
        in_specs=placed,
        out_specs=(P("tile", None), P(None, "tile", None)),
        check_vma=False,
    )
```

time: 510 us -> 64.5 us (0.13)
  waiting for transfers between devices: 183 us -> 0 us
  local copies, waits for them, and re-layouts: 142 us -> 10.3 us
  other arithmetic: 127 us -> 0 us
  Pallas kernels: 0 us -> 53.1 us
  starting transfers between devices: 42.7 us -> 0 us
  between operations: 14 us -> 0.66 us
    psum x4 -> x0, waiting for transfers between devices: 162 us -> none  [the longest x2 88.7 us: body(): adjoint = lax.psum(adjoint.reshape(2, rows, width), 'layer')]
    scatter-add x2 -> x0, other arithmetic: 108 us -> none  [body(): jnp.zeros((2, rows * width), jnp.float32).at[:, target].add(misfit)]
    gather x4 -> x0, local copies, waits for them, and re-layouts: 77.8 us -> none  [body(): picked = jnp.take(flat, target, axis=1)]
    pallas_call x0 -> x1, Pallas kernels: none -> 53.1 us  [body(): pl.pallas_call(functools.partial(kernel, n_tile, n_layer, groups), out_sh...]
    reshape x3 -> x0, local copies, waits for them, and re-layouts: 29.1 us -> none  [the longest x2 29 us: body(): adjoint = lax.psum(adjoint.reshape(2, rows, width), 'layer')]
    all_to_all x2 -> x0, starting transfers between devices: 24.6 us -> none  [the longest x1 14.6 us: body(): lax.all_to_all(obs_cells, 'tile', split_axis=2, concat_axis=0, tiled=True)]
    another operation x3 -> x0, local copies, waits for them, and re-layouts: 24.6 us -> none  [the longest x2 24.5 us: body(): speed = jnp.stack([speed[0] + scale * res_a, speed[1] + scale * res_b])]
    ppermute x8 -> x0, starting transfers between devices: 17.9 us -> none  [the longest x4 12.7 us: with_halo(): lax.ppermute(lax.slice_in_dim(block, block.shape[dim] - width, None, axis...]
  transfers between devices with their start and end apart: 14 -> 0, of which waited for: 9 -> 0; matrix products, arithmetic and copies ran while one was open for 2% -> 0% of each run, Pallas kernels for 0% -> 0%
where the time goes in v1:
time: 64.5 us; the launch traced here: 64.1 us
  Pallas kernels  53.1 us (82%)
  local copies, waits for them, and re-layouts  10.3 us (16%)
  between operations  0.66 us (1%)
    pallas_call x1, Pallas kernels, body(): pl.pallas_call(functools.partial(kernel, n_tile, n_layer, groups), out_sh...  53.1 us
    unnamed x22, local copies, waits for them, and re-layouts  10.3 us

profile of v1, /device:TPU:1, one launch (start us, length us, event | category | flops | bytes accessed | tf_op | source)
XLA Modules:
  0.0 64.1 jit_solution(10812139446991662531)
XLA Ops:
  0.6 0.0 copy-start.9
  0.6 0.6 %copy-done.9 = s32[1,1,64]{2,1,0:T(1,128)S(1)} copy-done((s32[1,1,64]{2,1,0:T(1,128)S(1)}, s32[1,1,64]{2,1,0:T(1,128)}, u32[]{:S(2)}) %copy-start.9) | copy-done | bytes 280
  1.3 0.0 copy-start
  1.3 1.1 %copy-done = f32[4,16,3072]{2,1,0:T(8,128)S(1)} copy-done((f32[4,16,3072]{2,1,0:T(8,128)S(1)}, f32[4,16,3072]{2,1,0:T(8,128)}, u32[]{:S(2)}) %copy-start) | copy-done | bytes 786456
  2.4 0.0 copy-start.1
  2.4 1.0 %copy-done.1 = f32[2,16,3072]{2,1,0:T(8,128)S(1)} copy-done((f32[2,16,3072]{2,1,0:T(8,128)S(1)}, f32[2,16,3072]{2,1,0:T(8,128)}, u32[]{:S(2)}) %copy-start.1) | copy-done | bytes 393240
  3.4 0.0 copy-start.2
  3.4 1.0 %copy-done.2 = f32[2,16,3072]{2,1,0:T(8,128)S(1)} copy-done((f32[2,16,3072]{2,1,0:T(8,128)S(1)}, f32[2,16,3072]{2,1,0:T(8,128)}, u32[]{:S(2)}) %copy-start.2) | copy-done | bytes 393240
  4.4 0.0 copy-start.3
  4.4 0.9 %copy-done.3 = f32[16,3072]{1,0:T(8,128)S(1)} copy-done((f32[16,3072]{1,0:T(8,128)S(1)}, f32[16,3072]{1,0:T(8,128)}, u32[]{:S(2)}) %copy-start.3) | copy-done | bytes 196632
  5.3 0.0 copy-start.4
  5.3 0.9 %copy-done.4 = f32[16,3072]{1,0:T(8,128)S(1)} copy-done((f32[16,3072]{1,0:T(8,128)S(1)}, f32[16,3072]{1,0:T(8,128)}, u32[]{:S(2)}) %copy-start.4) | copy-done | bytes 196632
  6.3 0.0 copy-start.5
  6.3 0.9 %copy-done.5 = s32[16,3072]{1,0:T(8,128)S(1)} copy-done((s32[16,3072]{1,0:T(8,128)S(1)}, s32[16,3072]{1,0:T(8,128)}, u32[]{:S(2)}) %copy-start.5) | copy-done | bytes 196632
  7.2 0.0 copy-start.6
  7.2 0.8 %copy-done.6 = f32[1,1,64,256]{3,2,1,0:T(8,128)S(1)} copy-done((f32[1,1,64,256]{3,2,1,0:T(8,128)S(1)}, f32[1,1,64,256]{3,2,1,0:T(8,128)}, u32[]{:S(2)}) %copy-start.6) | copy-done | bytes 65560
  8.0 0.0 copy-start.7
  8.0 0.8 %copy-done.7 = f32[1,1,64,128]{3,2,1,0:T(8,128)S(1)} copy-done((f32[1,1,64,128]{3,2,1,0:T(8,128)S(1)}, f32[1,1,64,128]{3,2,1,0:T(8,128)}, u32[]{:S(2)}) %copy-start.7) | copy-done | bytes 32792
  8.8 0.0 copy-start.8
  8.8 0.8 %copy-done.8 = s32[1,1,64,128]{3,2,1,0:T(8,128)S(1)} copy-done((s32[1,1,64,128]{3,2,1,0:T(8,128)S(1)}, s32[1,1,64,128]{3,2,1,0:T(8,128)}, u32[]{:S(2)}) %copy-start.8) | copy-done | bytes 32792
  9.6 53.1 %shard_map.113 = (f32[16,3072]{1,0:T(8,128)S(1)}, f32[2,16,3072]{2,1,0:T(8,128)S(1)}) custom-call(f32[2,16,3072]{2,1,0:T(8,128)S(1)} %copy-done.1, f32[16,3072]{1,0:T(8,128)S(1)} %copy-done.3, f32[16,3072]{1,0:T(8,128)S(1)} %copy-done.4, f32[4,16,3072]{2,1,0:T(8,128)S(1)} %copy-done, f32[2,16,3072]{2,1,0:T(8,128)S(1)} %copy-done.2, ...), custom_call_target="tpu_custom_call" | custom-call | tf_op jit(solution)/shard_map/pallas_call | solution.py:476
  62.6 0.7 %copy.14 = f32[16,3072]{1,0:T(8,128)} copy(f32[16,3072]{1,0:T(8,128)S(1)} %get-tuple-element.4) | data formatting | bytes 393216
  63.3 0.7 %copy.15 = f32[2,16,3072]{2,1,0:T(8,128)} copy(f32[2,16,3072]{2,1,0:T(8,128)S(1)} %get-tuple-element.5) | data formatting | bytes 786432
Async XLA Ops:
  0.6 0.7 %copy-start.9 = (s32[1,1,64]{2,1,0:T(1,128)S(1)}, s32[1,1,64]{2,1,0:T(1,128)}, u32[]{:S(2)}) copy-start(s32[1,1,64]{2,1,0:T(1,128)} %param.19) | copy-start | bytes 772
  1.3 1.1 %copy-start = (f32[4,16,3072]{2,1,0:T(8,128)S(1)}, f32[4,16,3072]{2,1,0:T(8,128)}, u32[]{:S(2)}) copy-start(f32[4,16,3072]{2,1,0:T(8,128)} %rate.1) | copy-start | bytes 2359300
  2.4 1.0 %copy-start.1 = (f32[2,16,3072]{2,1,0:T(8,128)S(1)}, f32[2,16,3072]{2,1,0:T(8,128)}, u32[]{:S(2)}) copy-start(f32[2,16,3072]{2,1,0:T(8,128)} %velocity.1) | copy-start | bytes 1179652
  3.4 1.0 %copy-start.2 = (f32[2,16,3072]{2,1,0:T(8,128)S(1)}, f32[2,16,3072]{2,1,0:T(8,128)}, u32[]{:S(2)}) copy-start(f32[2,16,3072]{2,1,0:T(8,128)} %driving.1) | copy-start | bytes 1179652
  4.4 0.9 %copy-start.3 = (f32[16,3072]{1,0:T(8,128)S(1)}, f32[16,3072]{1,0:T(8,128)}, u32[]{:S(2)}) copy-start(f32[16,3072]{1,0:T(8,128)} %friction.1) | copy-start | bytes 589828
  5.3 0.9 %copy-start.4 = (f32[16,3072]{1,0:T(8,128)S(1)}, f32[16,3072]{1,0:T(8,128)}, u32[]{:S(2)}) copy-start(f32[16,3072]{1,0:T(8,128)} %thickness.1) | copy-start | bytes 589828
  6.3 0.9 %copy-start.5 = (s32[16,3072]{1,0:T(8,128)S(1)}, s32[16,3072]{1,0:T(8,128)}, u32[]{:S(2)}) copy-start(s32[16,3072]{1,0:T(8,128)} %ice_mask.1) | copy-start | bytes 589828
  7.2 0.8 %copy-start.6 = (f32[1,1,64,256]{3,2,1,0:T(8,128)S(1)}, f32[1,1,64,256]{3,2,1,0:T(8,128)}, u32[]{:S(2)}) copy-start(f32[1,1,64,256]{3,2,1,0:T(8,128)} %param.16) | copy-start | bytes 196612
  8.0 0.8 %copy-start.7 = (f32[1,1,64,128]{3,2,1,0:T(8,128)S(1)}, f32[1,1,64,128]{3,2,1,0:T(8,128)}, u32[]{:S(2)}) copy-start(f32[1,1,64,128]{3,2,1,0:T(8,128)} %param.17) | copy-start | bytes 98308
  8.8 0.8 %copy-start.8 = (s32[1,1,64,128]{3,2,1,0:T(8,128)S(1)}, s32[1,1,64,128]{3,2,1,0:T(8,128)}, u32[]{:S(2)}) copy-start(s32[1,1,64,128]{3,2,1,0:T(8,128)} %param.18) | copy-start | bytes 98308

commit v2 on v1

--- a/solution.py
+++ b/solution.py
@@ -1,5 +1,4 @@
 import functools
-import math
 
 import jax
 import jax.numpy as jnp
@@ -12,6 +11,8 @@
 MESH = pl.DeviceIdType.MESH
 LANES = 128
 PIECES = 3
+VMEM_BYTES = 58 * 1024 * 1024
+
 CHANNELS = 3
 
 
@@ -25,9 +26,8 @@
 
 
 def kernel(
-    n_tile,
+    sides,
     n_layer,
-    groups,
     velocity,
     friction,
     thickness,
@@ -42,8 +42,8 @@
     velocity_out,
     packed,
     received,
-    left_side,
-    right_side,
+    left_sides,
+    right_sides,
     total,
     fields,
     from_sibling,
@@ -62,6 +62,10 @@
     col_send,
     col_recv,
     result,
+    seen_in,
+    weight_in,
+    cells_in,
+    counts_in,
     load_sems,
     obs_send_sem,
     obs_recv_sems,
@@ -77,6 +81,9 @@
     out_recv_sems,
     own_sems,
 ):
+    n_x, groups, n_y = sides
+    per_group = n_x * n_y
+    n_tile = groups * per_group
     t = lax.axis_index("tile")
     l = lax.axis_index("layer")
     rows, width = friction.shape
@@ -84,7 +91,6 @@
     depth = rate.shape[0]
     total_layers = depth * n_layer
     slots = obs_weight.shape[-1]
-    per_group = n_tile // groups
     marks = rows * n_layer
     core = lax.rem(l, 2)
     pair = l // 2
@@ -120,15 +126,30 @@
         pltpu.make_async_copy(
             rate.at[:, :, columns], rates.at[pl.ds(l * depth, depth)], load_sems.at[7]
         ),
+        pltpu.make_async_copy(obs_velocity, seen_in, load_sems.at[8]),
+        pltpu.make_async_copy(obs_weight, weight_in, load_sems.at[9]),
+        pltpu.make_async_copy(obs_cells, cells_in, load_sems.at[10]),
+        pltpu.make_async_copy(obs_counts, counts_in, load_sems.at[11]),
     ]
     for load in loads:
         load.start()
 
     barrier = pltpu.get_barrier_semaphore()
 
-    def greet(offset, carry):
+    x, z, y = t // (groups * n_y), lax.rem(t // n_y, groups), lax.rem(t, n_y)
+
+    def peer(turn):
+        ring = turn // per_group
+        step = lax.rem(ring, 2)
+        hop = step * ((ring + 1) // 2) + (1 - step) * (groups - ring // 2)
+        to_x = lax.rem(x + lax.rem(turn // n_y, n_x), n_x)
+        to_z = lax.rem(z + hop, groups)
+        to_y = lax.rem(y + turn, n_y)
+        return (to_x * groups + to_z) * n_y + to_y
+
+    def greet(turn, carry):
         pl.semaphore_signal(
-            barrier, inc=1, device_id=(lax.rem(t + offset, n_tile), l), device_id_type=MESH
+            barrier, inc=1, device_id=(peer(n_tile - turn), l), device_id_type=MESH
         )
         return carry
 
@@ -138,18 +159,19 @@
             barrier, inc=1, device_id=(t, lax.rem(l + offset, n_layer)), device_id_type=MESH
         )
 
+    for load in loads[8:]:
+        load.wait()
     row_id = lax.broadcasted_iota(jnp.int32, (n_tile, n_tile), 0)
     col_id = lax.broadcasted_iota(jnp.int32, (n_tile, n_tile), 1)
     counts = jnp.sum(
-        jnp.where(row_id == col_id, obs_counts[...].astype(jnp.float32), 0.0), axis=1, keepdims=True
+        jnp.where(row_id == col_id, counts_in[...].astype(jnp.float32), 0.0), axis=1, keepdims=True
     )
     place = lax.broadcasted_iota(jnp.int32, (n_tile, slots), 1).astype(jnp.float32)
-    weight = jnp.where(place < counts, obs_weight[...], 0.0)
+    weight = jnp.where(place < counts, weight_in[...], 0.0)
     packed[:, 0, :] = weight
-    packed[:, 1, :] = weight * obs_velocity[:, :slots]
-    packed[:, 2, :] = weight * obs_velocity[:, slots:]
-    packed[:, 3, :] = obs_cells[...].astype(jnp.float32)
-    received[0] = packed[t]
+    packed[:, 1, :] = weight * seen_in[:, :slots]
+    packed[:, 2, :] = weight * seen_in[:, slots:]
+    packed[:, 3, :] = cells_in[...].astype(jnp.float32)
 
     for load in loads[:3]:
         load.wait()
@@ -214,44 +236,51 @@
 
     first_rows = swap_rows(0)
 
-    def send_obs(offset, carry):
-        to = lax.rem(t + offset, n_tile)
+    own_block = pltpu.make_async_copy(packed.at[t], received.at[0], obs_recv_sems.at[0])
+    own_block.start()
+
+    def send_obs(turn, carry):
+        to = peer(turn)
         remote(
             packed.at[to],
-            received.at[offset],
+            received.at[turn],
             obs_send_sem,
-            obs_recv_sems.at[offset // per_group],
+            obs_recv_sems.at[turn // per_group],
             to,
             l,
         ).start()
         return carry
 
+    def send_rates():
+        copies = []
+        for offset in (2, 3, 1):
+            to = lax.rem(l + offset, n_layer)
+            copy = remote(
+                rate.at[:, :, pl.ds(pl.multiple_of(to * quarter, LANES), quarter)],
+                rates.at[pl.ds(l * depth, depth)],
+                rate_send_sems.at[offset - 1],
+                rate_recv_sems.at[offset - 1],
+                t,
+                to,
+            )
+            copy.start()
+            copies.append(copy)
+        return copies
+
     lax.fori_loop(1, n_tile, send_obs, 0)
-
-    rate_copies = []
-    for offset in (1, 2, 3):
-        to = lax.rem(l + offset, n_layer)
-        copy = remote(
-            rate.at[:, :, pl.ds(pl.multiple_of(to * quarter, LANES), quarter)],
-            rates.at[pl.ds(l * depth, depth)],
-            rate_send_sems.at[offset - 1],
-            rate_recv_sems.at[offset - 1],
-            t,
-            to,
-        )
-        copy.start()
-        rate_copies.append(copy)
+    rate_copies = send_rates()
 
     total[...] = jnp.zeros_like(total)
     mark_id = lax.broadcasted_iota(jnp.int32, (marks, slots), 0).astype(jnp.float32)
     lane_id = lax.broadcasted_iota(jnp.int32, (slots, quarter), 1).astype(jnp.float32)
 
-    def gather_group(group, count, start):
-        return pltpu.make_async_copy(
-            received.at[pl.ds(start, count)], received.at[pl.ds(start, count)], obs_recv_sems.at[group]
-        )
-
-    def add_group(group):
+    def build(group, left_side, right_side):
+        start = group * per_group
+        pltpu.make_async_copy(
+            received.at[pl.ds(start, per_group)],
+            received.at[pl.ds(start, per_group)],
+            obs_recv_sems.at[group],
+        ).wait()
         block = received[pl.ds(group * per_group, per_group)]
         cell = block[:, 3, :]
         mark = jnp.floor((cell + 0.5) * (1.0 / quarter))
@@ -271,39 +300,22 @@
             right_side[b * slots : (b + 1) * slots, :] = jnp.where(
                 column[:, b : b + 1] == lane_id, 1.0, 0.0
             ).astype(jnp.bfloat16)
+
+    def multiply(left_side, right_side):
         total[...] += jnp.dot(left_side[...], right_side[...], preferred_element_type=jnp.float32)
 
-    gather_group(0, per_group - 1, 1).wait()
-    add_group(0)
-
-    def later_group(group, carry):
-        gather_group(group, per_group, group * per_group).wait()
-        add_group(group)
+    even, odd = (left_sides[0], right_sides[0]), (left_sides[1], right_sides[1])
+
+    def two_groups(pair, carry):
+        build(2 * pair + 1, *odd)
+        multiply(*even)
+        build(2 * pair + 2, *even)
+        multiply(*odd)
         return carry
 
-    lax.fori_loop(1, groups, later_group, 0)
-
-    def collect(q):
-        for channel in range(CHANNELS):
-            field = None
-            for piece in range(PIECES):
-                start = pl.multiple_of((channel * PIECES + piece) * marks + q * rows, rows)
-                part = total[pl.ds(start, rows), :]
-                field = part if field is None else field + part
-            fields[q, channel] = field
-
-    sum_copies = []
-    for k, chip in enumerate((1 - pair, pair)):
-        q = chip * 2 + (1 - core)
-        collect(q)
-        copy = remote(
-            fields.at[q], from_sibling.at[k], sum_send_sems.at[k], sum_recv_sems.at[k], t, sibling
-        )
-        copy.start()
-        sum_copies.append(copy)
-    collect(partner)
-
-    for load in loads[3:]:
+    build(0, *even)
+    lax.fori_loop(0, groups // 2 - 1, two_groups, 0)
+    for load in loads[3:8]:
         load.wait()
     for copy in rate_copies:
         copy.wait()
@@ -387,6 +399,30 @@
     stress = stresses(strain, visc)
     edges = send_edges(1, (stress[0], stress[2]), (stress[2], stress[1]))
 
+    build(groups - 1, *odd)
+    multiply(*even)
+    multiply(*odd)
+
+    def collect(q):
+        for channel in range(CHANNELS):
+            field = None
+            for piece in range(PIECES):
+                start = pl.multiple_of((channel * PIECES + piece) * marks + q * rows, rows)
+                part = total[pl.ds(start, rows), :]
+                field = part if field is None else field + part
+            fields[q, channel] = field
+
+    sum_copies = []
+    for k, chip in enumerate((1 - pair, pair)):
+        q = chip * 2 + (1 - core)
+        collect(q)
+        copy = remote(
+            fields.at[q], from_sibling.at[k], sum_send_sems.at[k], sum_recv_sems.at[k], t, sibling
+        )
+        copy.start()
+        sum_copies.append(copy)
+    collect(partner)
+
     sum_copies[0].wait()
     pair_sum[...] = fields[partner] + from_sibling[0]
     cross = remote(pair_sum, from_partner, sum_send_sems.at[2], sum_recv_sems.at[2], t, partner)
@@ -424,25 +460,31 @@
     result[1] = speed[1]
     result[2] = new_coeff(coeff, fric, speed)
 
-    finals = [
+    own = [
         pltpu.make_async_copy(result.at[0:2], velocity_out.at[:, :, columns], own_sems.at[0]),
         pltpu.make_async_copy(result.at[2], friction_out.at[:, columns], own_sems.at[1]),
     ]
-    for copy in finals:
+    other = pl.ds(pl.multiple_of(partner * quarter, LANES), quarter)
+    sent, crossed, passed = [], [], []
+    for k, src in enumerate((result.at[0], result.at[1], result.at[2])):
+        dst = friction_out.at[:, columns] if k == 2 else velocity_out.at[k, :, columns]
+        copy = remote(src, dst, out_send_sems.at[0, k], out_recv_sems.at[0, k], t, partner)
         copy.start()
-    for offset in (1, 2, 3):
-        to = lax.rem(l + offset, n_layer)
-        pairs = (
-            (result.at[0:2], velocity_out.at[:, :, columns]),
-            (result.at[2], friction_out.at[:, columns]),
-        )
-        for k, (src, dst) in enumerate(pairs):
-            copy = remote(
-                src, dst, out_send_sems.at[offset - 1, k], out_recv_sems.at[offset - 1, k], t, to
-            )
-            copy.start()
-            finals.append(copy)
-    for copy in finals:
+        crossed.append(copy)
+        copy = remote(src, dst, out_send_sems.at[1, k], out_recv_sems.at[1, k], t, sibling)
+        copy.start()
+        sent.append(copy)
+    for copy in own:
+        copy.start()
+    for k, copy in enumerate(crossed):
+        copy.wait_recv()
+        dst = friction_out.at[:, other] if k == 2 else velocity_out.at[k, :, other]
+        copy = remote(dst, dst, out_send_sems.at[2, k], out_recv_sems.at[2, k], t, sibling)
+        copy.start()
+        passed.append(copy)
+    for copy in crossed:
+        copy.wait_send()
+    for copy in own + sent + passed:
         copy.wait()
 
     pltpu.make_async_copy(
@@ -467,25 +509,25 @@
     quarter = width // n_layer
     slots = obs_weight.shape[-1]
     depth = rate.shape[0]
-    groups = 8 if n_tile % 8 == 0 else 2
+    sides = (4, n_tile // 8, 2) if n_tile % 8 == 0 else (1, n_tile // 2, 2)
     marks = rows * n_layer
+    groups = sides[1]
     chunk = (n_tile // groups) * slots
-    anywhere = pl.BlockSpec(memory_space=pl.ANY)
-    in_vmem = pl.BlockSpec(memory_space=pltpu.VMEM)
+    in_hbm = pl.BlockSpec(memory_space=pltpu.HBM)
     f32 = jnp.float32
     friction_out, velocity_out = pl.pallas_call(
-        functools.partial(kernel, n_tile, n_layer, groups),
+        functools.partial(kernel, sides, n_layer),
         out_shape=(
             jax.ShapeDtypeStruct(friction.shape, f32),
             jax.ShapeDtypeStruct(velocity.shape, f32),
         ),
-        in_specs=[anywhere] * 6 + [in_vmem] * 4,
-        out_specs=(anywhere, anywhere),
+        in_specs=[in_hbm] * 10,
+        out_specs=(in_hbm, in_hbm),
         scratch_shapes=[
             pltpu.VMEM((n_tile, 4, slots), f32),
             pltpu.VMEM((n_tile, 4, slots), f32),
-            pltpu.VMEM((CHANNELS * PIECES * marks, chunk), jnp.bfloat16),
-            pltpu.VMEM((chunk, quarter), jnp.bfloat16),
+            [pltpu.VMEM((CHANNELS * PIECES * marks, chunk), jnp.bfloat16)] * 2,
+            [pltpu.VMEM((chunk, quarter), jnp.bfloat16)] * 2,
             pltpu.VMEM((CHANNELS * PIECES * marks, quarter), f32),
             pltpu.VMEM((n_layer, CHANNELS, rows, quarter), f32),
             pltpu.VMEM((2, CHANNELS, rows, quarter), f32),
@@ -504,7 +546,11 @@
             pltpu.VMEM((3, 2, 2, rows, LANES), f32),
             pltpu.VMEM((3, 2, 2, rows, LANES), f32),
             pltpu.VMEM((3, rows, quarter), f32),
-            pltpu.SemaphoreType.DMA((8,)),
+            pltpu.VMEM((n_tile, 2 * slots), f32),
+            pltpu.VMEM((n_tile, slots), f32),
+            pltpu.VMEM((n_tile, slots), jnp.int32),
+            pltpu.VMEM((1, n_tile), jnp.int32),
+            pltpu.SemaphoreType.DMA((12,)),
             pltpu.SemaphoreType.DMA,
             pltpu.SemaphoreType.DMA((groups,)),
             pltpu.SemaphoreType.DMA((3,)),
@@ -515,12 +561,12 @@
             pltpu.SemaphoreType.DMA((3, 2)),
             pltpu.SemaphoreType.DMA((3,)),
             pltpu.SemaphoreType.DMA((3,)),
-            pltpu.SemaphoreType.DMA((3, 2)),
-            pltpu.SemaphoreType.DMA((3, 2)),
+            pltpu.SemaphoreType.DMA((3, 3)),
+            pltpu.SemaphoreType.DMA((3, 3)),
             pltpu.SemaphoreType.DMA((2,)),
         ],
         compiler_params=pltpu.CompilerParams(
-            collective_id=0, has_side_effects=True, vmem_limit_bytes=40 * 1024 * 1024
+            collective_id=0, has_side_effects=True, vmem_limit_bytes=VMEM_BYTES
         ),
     )(
         velocity,

time: 64.5 us -> 52.5 us (0.81)
  local copies, waits for them, and re-layouts: 10.3 us -> 2.42 us
  Pallas kernels: 53.1 us -> 49.3 us
    unnamed x22 -> x4, local copies, waits for them, and re-layouts: 10.3 us -> 2.42 us
    pallas_call x1, Pallas kernels: 53.1 us -> 49.3 us  [body(): pl.pallas_call(functools.partial(kernel, sides, n_layer), out_shape=(jax....]
where the time goes in v2:
time: 52.5 us; the launch traced here: 52.4 us
  Pallas kernels  49.3 us (94%)
  local copies, waits for them, and re-layouts  2.42 us (5%)
  between operations  0.65 us (1%)
    pallas_call x1, Pallas kernels, body(): pl.pallas_call(functools.partial(kernel, sides, n_layer), out_shape=(jax....  49.3 us
    unnamed x4, local copies, waits for them, and re-layouts  2.42 us

profile of v2, /device:TPU:1, one launch (start us, length us, event | category | flops | bytes accessed | tf_op | source)
XLA Modules:
  0.0 52.4 jit_solution(14200723304924442903)
XLA Ops:
  0.6 49.3 %shard_map.113 = (f32[16,3072]{1,0:T(8,128)}, f32[2,16,3072]{2,1,0:T(8,128)}) custom-call(f32[2,16,3072]{2,1,0:T(8,128)} %velocity.1, f32[16,3072]{1,0:T(8,128)} %friction.1, f32[16,3072]{1,0:T(8,128)} %thickness.1, f32[4,16,3072]{2,1,0:T(8,128)} %rate.1, f32[2,16,3072]{2,1,0:T(8,128)} %driving.1, s32[16,3072]{1,0:T(8,128)} %ice_mask.1, f32[64,256]{1,0:T(8,128)} %bitcast.4, ...), custom_call_target="tpu_custom_call" | custom-call | tf_op jit(solution)/shard_map/pallas_call | solution.py:518
  49.9 0.0 copy-start
  49.9 1.7 %copy.14 = f32[16,3072]{1,0:T(8,128)} copy(f32[16,3072]{1,0:T(8,128)} %get-tuple-element.4) | data formatting | bytes 393216
  51.6 0.0 copy-done
  51.6 0.7 %copy.15 = f32[2,16,3072]{2,1,0:T(8,128)} copy(f32[2,16,3072]{2,1,0:T(8,128)S(1)} %copy-done) | data formatting | bytes 786432
Async XLA Ops:
  49.9 1.7 %copy-start = (f32[2,16,3072]{2,1,0:T(8,128)S(1)}, f32[2,16,3072]{2,1,0:T(8,128)}, u32[]{:S(2)}) copy-start(f32[2,16,3072]{2,1,0:T(8,128)} %get-tuple-element.5) | copy-start | bytes 1179652

commit v3 on v2

v3 whole, which is shorter than its diff:
```python
import functools

import jax
import jax.numpy as jnp
from jax import lax
from jax.experimental import pallas as pl
from jax.experimental.pallas import tpu as pltpu
from jax.sharding import PartitionSpec as P

ITERS = 2
MESH = pl.DeviceIdType.MESH
LANES = 128
PIECES = 3
VMEM_BYTES = 58 * 1024 * 1024
IT1_AT = 1

CHANNELS = 3


def split_pieces(value):
    pieces = []
    for _ in range(PIECES):
        piece = value.astype(jnp.bfloat16).astype(jnp.float32)
        pieces.append(piece)
        value = value - piece
    return pieces


def kernel(
    sides,
    n_layer,
    velocity,
    friction,
    thickness,
    rate,
    driving,
    ice_mask,
    obs_velocity,
    obs_weight,
    obs_cells,
    obs_counts,
    friction_out,
    velocity_out,
    packed,
    received,
    left_sides,
    right_sides,
    total,
    fields,
    from_sibling,
    chip_sum,
    other_sum,
    along_send,
    along_recv,
    rates,
    vel,
    edge,
    fric_in,
    thick,
    drive,
    mask,
    part_send,
    part_recv,
    row_send,
    row_recv,
    col_send,
    col_recv,
    result,
    seen_in,
    weight_in,
    cells_in,
    counts_in,
    load_sems,
    obs_send_sem,
    obs_recv_sems,
    rate_sems,
    part_send_sems,
    part_recv_sems,
    row_send_sems,
    row_recv_sems,
    col_send_sems,
    col_recv_sems,
    sum_send_sems,
    sum_recv_sems,
    out_send_sems,
    out_recv_sems,
    own_sems,
):
    n_x, groups, n_y = sides
    per_group = n_x * n_y
    n_tile = groups * per_group
    t = lax.axis_index("tile")
    l = lax.axis_index("layer")
    rows, width = friction.shape
    half = width // 2
    quarter = width // n_layer
    depth = rate.shape[0]
    total_layers = depth * n_layer
    slots = obs_weight.shape[-1]
    marks = rows * n_layer
    core = lax.rem(l, 2)
    chip = l // 2
    sibling = chip * 2 + (1 - core)
    partner = (1 - chip) * 2 + core
    across = (1 - chip) * 2 + (1 - core)
    above = lax.rem(t + n_tile - 1, n_tile)
    below = lax.rem(t + 1, n_tile)
    first = pl.multiple_of(core * half, LANES)
    columns = pl.ds(first, half)
    sibling_columns = pl.ds(pl.multiple_of((1 - core) * half, LANES), half)

    def remote(src, dst, send_sem, recv_sem, tile, layer):
        return pltpu.make_async_remote_copy(
            src_ref=src,
            dst_ref=dst,
            send_sem=send_sem,
            recv_sem=recv_sem,
            device_id=(tile, layer),
            device_id_type=MESH,
        )

    beside = pl.multiple_of(half - LANES * core, LANES)
    loads = [
        pltpu.make_async_copy(obs_velocity, seen_in, load_sems.at[0]),
        pltpu.make_async_copy(obs_weight, weight_in, load_sems.at[1]),
        pltpu.make_async_copy(obs_cells, cells_in, load_sems.at[2]),
        pltpu.make_async_copy(obs_counts, counts_in, load_sems.at[3]),
        pltpu.make_async_copy(velocity.at[:, :, columns], vel, load_sems.at[4]),
        pltpu.make_async_copy(velocity.at[:, :, pl.ds(beside, LANES)], edge, load_sems.at[5]),
        pltpu.make_async_copy(friction.at[:, columns], fric_in, load_sems.at[6]),
        pltpu.make_async_copy(thickness.at[:, columns], thick, load_sems.at[7]),
        pltpu.make_async_copy(driving.at[:, :, columns], drive, load_sems.at[8]),
        pltpu.make_async_copy(ice_mask.at[:, columns], mask, load_sems.at[9]),
        pltpu.make_async_copy(
            rate.at[:, :, columns], rates.at[pl.ds(core * depth, depth)], load_sems.at[10]
        ),
    ]
    for load in loads:
        load.start()

    barrier = pltpu.get_barrier_semaphore()
    x, z, y = t // (groups * n_y), lax.rem(t // n_y, groups), lax.rem(t, n_y)

    def peer(turn):
        ring = turn // per_group
        step = lax.rem(ring, 2)
        hop = step * ((ring + 1) // 2) + (1 - step) * (groups - ring // 2)
        to_x = lax.rem(x + lax.rem(turn // n_y, n_x), n_x)
        to_z = lax.rem(z + hop, groups)
        to_y = lax.rem(y + turn, n_y)
        return (to_x * groups + to_z) * n_y + to_y

    def greet_one(tile, layer):
        pl.semaphore_signal(barrier, inc=1, device_id=(tile, layer), device_id_type=MESH)

    def greet(turn, carry):
        greet_one(peer(n_tile - turn), l)
        return carry

    lax.fori_loop(1, n_tile, greet, 0)
    greet_one(above, partner)
    greet_one(below, partner)
    for layer in (partner, across, sibling):
        greet_one(t, layer)

    for load in loads[:4]:
        load.wait()
    row_id = lax.broadcasted_iota(jnp.int32, (n_tile, n_tile), 0)
    col_id = lax.broadcasted_iota(jnp.int32, (n_tile, n_tile), 1)
    counts = jnp.sum(
        jnp.where(row_id == col_id, counts_in[...].astype(jnp.float32), 0.0), axis=1, keepdims=True
    )
    place = lax.broadcasted_iota(jnp.int32, (n_tile, slots), 1).astype(jnp.float32)
    weight = jnp.where(place < counts, weight_in[...], 0.0)
    packed[:, 0, :] = weight
    packed[:, 1, :] = weight * seen_in[:, :slots]
    packed[:, 2, :] = weight * seen_in[:, slots:]
    packed[:, 3, :] = cells_in[...].astype(jnp.float32)

    for load in loads[4:6]:
        load.wait()
    row_send[0, 0] = vel[:, 0, :]
    row_send[0, 1] = vel[:, rows - 1, :]

    pl.semaphore_wait(barrier, n_tile - 1 + 2 + n_layer - 1)

    def row_copies(phase):
        copies = []
        for side, tile in ((0, above), (1, below)):
            for source, layer in enumerate((l, partner) if phase % 2 else (l,)):
                copies.append(
                    remote(
                        row_send.at[phase, side],
                        row_recv.at[phase, 1 - side, source],
                        row_send_sems.at[phase, side, source],
                        row_recv_sems.at[phase, 1 - side, source],
                        tile,
                        layer,
                    )
                )
        return copies

    def col_copies(phase):
        return [
            remote(
                col_send.at[phase - 1],
                col_recv.at[phase - 1, source],
                col_send_sems.at[phase - 1, source],
                col_recv_sems.at[phase - 1, source],
                t,
                layer,
            )
            for source, layer in enumerate((sibling, across) if phase % 2 else (sibling,))
        ]

    def part_copy(turn):
        return remote(
            part_send.at[turn],
            part_recv.at[turn],
            part_send_sems.at[turn],
            part_recv_sems.at[turn],
            t,
            partner,
        )

    def start(copies):
        for copy in copies:
            copy.start()

    def wait(copies):
        for copy in copies:
            copy.wait()

    start(row_copies(0))
    own_block = pltpu.make_async_copy(packed.at[t], received.at[0], obs_recv_sems.at[0])
    own_block.start()

    def send_obs(turn, carry):
        to = peer(turn)
        remote(
            packed.at[to],
            received.at[turn],
            obs_send_sem,
            obs_recv_sems.at[turn // per_group],
            to,
            l,
        ).start()
        return carry

    lax.fori_loop(1, n_tile, send_obs, 0)
    rate_copy = remote(
        rate.at[:, :, sibling_columns],
        rates.at[pl.ds(core * depth, depth)],
        rate_sems.at[0],
        rate_sems.at[1],
        t,
        sibling,
    )
    rate_copy.start()

    row_of = lax.broadcasted_iota(jnp.int32, (rows, half), 0)
    col_of = lax.broadcasted_iota(jnp.int32, (rows, half), 1)
    top, bottom = t == 0, t == n_tile - 1
    at_left = core == 0

    def diff_rows(field, low, high):
        low = jnp.where(top, 0.0, low)
        high = jnp.where(bottom, 0.0, high)
        previous = jnp.where(row_of == 0, low, pltpu.roll(field, 1, 0))
        following = jnp.where(row_of == rows - 1, high, pltpu.roll(field, rows - 1, 0))
        return 0.5 * (following - previous)

    def diff_cols(field, tile):
        low = jnp.where(at_left, 0.0, tile[:, LANES - 1 : LANES])
        high = jnp.where(at_left, tile[:, 0:1], 0.0)
        previous = jnp.where(col_of == 0, low, pltpu.roll(field, 1, 1))
        following = jnp.where(col_of == half - 1, high, pltpu.roll(field, half - 1, 1))
        return 0.5 * (following - previous)

    def row_halo(phase, k):
        low, high = row_recv[phase, 0, 0, k : k + 1, :], row_recv[phase, 1, 0, k : k + 1, :]
        if phase % 2:
            low = low + row_recv[phase, 0, 1, k : k + 1, :]
            high = high + row_recv[phase, 1, 1, k : k + 1, :]
        return low, high

    def col_halo(phase, k):
        tile = col_recv[phase - 1, 0, k]
        return tile + col_recv[phase - 1, 1, k] if phase % 2 else tile

    def stage(phase, by_row, by_col):
        for k in range(2):
            row_send[phase, 0, k : k + 1, :] = by_row[k][0:1, :]
            row_send[phase, 1, k : k + 1, :] = by_row[k][rows - 1 : rows, :]
            col_send[phase - 1, k] = jnp.where(
                at_left, by_col[k][:, half - LANES :], by_col[k][:, :LANES]
            )

    def strains(speed, phase, tiles):
        exx = diff_rows(speed[0], *row_halo(phase, 0))
        eyy = diff_cols(speed[1], tiles[1])
        exy = 0.5 * (diff_cols(speed[0], tiles[0]) + diff_rows(speed[1], *row_halo(phase, 1)))
        return exx, eyy, exy

    def stresses(strain, visc):
        exx, eyy, exy = strain
        return 2.0 * visc * (2.0 * exx + eyy), 2.0 * visc * (2.0 * eyy + exx), 2.0 * visc * exy

    chip_layers = 2 * depth
    first_layer = (chip * chip_layers).astype(jnp.float32)

    def send_part(turn, strain, speed, fric):
        exx, eyy, exy = strain
        e2 = exx * exx + eyy * eyy + exx * eyy + exy * exy + 0.05
        b2 = 0.25 * fric * fric * (speed[0] * speed[0] + speed[1] * speed[1])
        layer_sum = jnp.zeros_like(e2)
        for k in range(chip_layers):
            height = 1.0 - (first_layer + (k + 0.5)) * (1.0 / total_layers)
            layer_sum = layer_sum + rates[k] * jnp.exp(
                jnp.log(e2 + (height * height) * b2) * (-1.0 / 3.0)
            )
        part = thick[...] * (layer_sum * (1.0 / total_layers))
        part_send[turn] = part
        sxx, syy, sxy = stresses(strain, part)
        phase = 2 * turn + 1
        stage(phase, (sxx, sxy), (sxy, syy))
        start(row_copies(phase))
        part_copy(turn).start()
        start(col_copies(phase))

    def new_speed(turn, strain, speed, fric):
        phase = 2 * turn + 1
        wait(row_copies(phase) + [part_copy(turn)] + col_copies(phase))
        visc = part_send[turn] + part_recv[turn]
        sxx, syy, sxy = stresses(strain, visc)
        div_0 = diff_rows(sxx, *row_halo(phase, 0)) + diff_cols(sxy, col_halo(phase, 0))
        div_1 = diff_rows(sxy, *row_halo(phase, 1)) + diff_cols(syy, col_halo(phase, 1))
        icy = jnp.where(mask[...] >= 1, 1.0, 0.0)
        scale = 0.5 * icy / (1.0 + fric + 4.0 * visc)
        return (
            speed[0] + scale * (div_0 - fric * speed[0] + drive[0]),
            speed[1] + scale * (div_1 - fric * speed[1] + drive[1]),
        )

    def drag(coeff):
        return jnp.where(mask[...] == 2, 1.0, 0.0) * jnp.exp(coeff)

    def first_state():
        speed = (vel[0], vel[1])
        return strains(speed, 0, (edge[0], edge[1])), speed, drag(fric_in[...])

    def first_part():
        wait(loads[6:])
        rate_copy.wait()
        wait(row_copies(0))
        send_part(0, *first_state())

    total[...] = jnp.zeros_like(total)
    mark_id = lax.broadcasted_iota(jnp.int32, (marks, slots), 0).astype(jnp.float32)
    lane_id = lax.broadcasted_iota(jnp.int32, (slots, quarter), 1).astype(jnp.float32)

    def arrive(group):
        blocks = received.at[pl.ds(group * per_group, per_group)]
        pltpu.make_async_copy(blocks, blocks, obs_recv_sems.at[group]).wait()

    def build(group, left_side, right_side):
        block = received[pl.ds(group * per_group, per_group)]
        cell = block[:, 3, :]
        mark = jnp.floor((cell + 0.5) * (1.0 / quarter))
        column = cell - mark * quarter
        row = jnp.floor((mark + 0.5) * (1.0 / n_layer))
        mark = (mark - row * n_layer) * rows + row
        column = column.T
        pieces = []
        for channel in range(CHANNELS):
            pieces += split_pieces(block[:, channel, :])
        for b in range(per_group):
            hit = mark[b : b + 1, :] == mark_id
            for p, piece in enumerate(pieces):
                left_side[p * marks : (p + 1) * marks, b * slots : (b + 1) * slots] = jnp.where(
                    hit, piece[b : b + 1, :], 0.0
                ).astype(jnp.bfloat16)
            right_side[b * slots : (b + 1) * slots, :] = jnp.where(
                column[:, b : b + 1] == lane_id, 1.0, 0.0
            ).astype(jnp.bfloat16)

    def multiply(left_side, right_side):
        total[...] += jnp.dot(left_side[...], right_side[...], preferred_element_type=jnp.float32)

    even, odd = (left_sides[0], right_sides[0]), (left_sides[1], right_sides[1])
    turns = groups // 2

    def two_groups(turn, carry):
        arrive(2 * turn + 1)
        pl.when(turn < turns - 1)(lambda: arrive(2 * turn + 2))
        pl.when(turn == min(IT1_AT, turns - 1))(first_part)
        build(2 * turn + 1, *odd)
        multiply(*even)
        build(lax.rem(2 * turn + 2, groups), *even)
        multiply(*odd)
        return carry

    arrive(0)
    build(0, *even)
    lax.fori_loop(0, turns, two_groups, 0)

    def collect(side):
        for channel in range(CHANNELS):
            for q in range(2):
                field = None
                for piece in range(PIECES):
                    at = (channel * PIECES + piece) * marks + (side * 2 + q) * rows
                    part = total[pl.ds(pl.multiple_of(at, rows), rows), :]
                    field = part if field is None else field + part
                fields[side, channel, :, q * quarter : (q + 1) * quarter] = field

    collect(1 - core)
    sum_copy = remote(
        fields.at[1 - core], from_sibling, sum_send_sems.at[0], sum_recv_sems.at[0], t, sibling
    )
    sum_copy.start()
    collect(core)

    strain, speed, fric = first_state()
    speed = new_speed(0, strain, speed, fric)
    stage(2, speed, speed)
    swaps = row_copies(2) + col_copies(2)
    start(swaps)

    def misfit(sums, speed):
        return speed[0] * (sums[0] * speed[0] - sums[1]) + speed[1] * (
            sums[0] * speed[1] - sums[2]
        )

    sum_copy.wait()
    sums = [fields[core, k] + from_sibling[k] for k in range(CHANNELS)]
    for k in range(CHANNELS):
        chip_sum[k] = sums[k]
    along_send[...] = misfit(sums, speed)
    along_copy = remote(
        along_send, along_recv, sum_send_sems.at[1], sum_recv_sems.at[1], t, partner
    )
    along_copy.start()
    chip_copy = remote(chip_sum, other_sum, sum_send_sems.at[2], sum_recv_sems.at[2], t, partner)
    chip_copy.start()
    wait(swaps)
    strain = strains(speed, 2, (col_halo(2, 0), col_halo(2, 1)))
    along_copy.wait()
    coeff = fric_in[...] - 0.2 * fric * (along_send[...] + along_recv[...])

    fric = drag(coeff)
    send_part(1, strain, speed, fric)
    speed = new_speed(1, strain, speed, fric)
    result[0] = speed[0]
    result[1] = speed[1]
    chip_copy.wait()
    sums = [chip_sum[k] + other_sum[k] for k in range(CHANNELS)]
    result[2] = coeff - 0.2 * fric * misfit(sums, speed)

    finals = []
    for k, dst in ((0, velocity_out.at[:, :, columns]), (1, friction_out.at[:, columns])):
        src = result.at[0:2] if k == 0 else result.at[2]
        finals.append(
            remote(src, dst, out_send_sems.at[k], out_recv_sems.at[k], t, sibling)
        )
        finals.append(pltpu.make_async_copy(src, dst, own_sems.at[k]))
    start(finals)
    wait(finals)

    blocks = packed.at[pl.ds(1, n_tile - 1)]
    pltpu.make_async_copy(blocks, blocks, obs_send_sem).wait()


def body(
    velocity,
    friction,
    thickness,
    rate,
    driving,
    ice_mask,
    obs_velocity,
    obs_weight,
    obs_cells,
    obs_counts,
):
    n_tile, n_layer = lax.axis_size("tile"), lax.axis_size("layer")
    rows, width = friction.shape
    half, quarter = width // 2, width // n_layer
    slots = obs_weight.shape[-1]
    depth = rate.shape[0]
    sides = (4, n_tile // 8, 2) if n_tile % 8 == 0 else (1, n_tile // 2, 2)
    marks = rows * n_layer
    groups = sides[1]
    chunk = (n_tile // groups) * slots
    in_hbm = pl.BlockSpec(memory_space=pltpu.HBM)
    f32 = jnp.float32
    friction_out, velocity_out = pl.pallas_call(
        functools.partial(kernel, sides, n_layer),
        out_shape=(
            jax.ShapeDtypeStruct(friction.shape, f32),
            jax.ShapeDtypeStruct(velocity.shape, f32),
        ),
        in_specs=[in_hbm] * 10,
        out_specs=(in_hbm, in_hbm),
        scratch_shapes=[
            pltpu.VMEM((n_tile, 4, slots), f32),
            pltpu.VMEM((n_tile, 4, slots), f32),
            [pltpu.VMEM((CHANNELS * PIECES * marks, chunk), jnp.bfloat16)] * 2,
            [pltpu.VMEM((chunk, quarter), jnp.bfloat16)] * 2,
            pltpu.VMEM((CHANNELS * PIECES * marks, quarter), f32),
            pltpu.VMEM((2, CHANNELS, rows, half), f32),
            pltpu.VMEM((CHANNELS, rows, half), f32),
            pltpu.VMEM((CHANNELS, rows, half), f32),
            pltpu.VMEM((CHANNELS, rows, half), f32),
            pltpu.VMEM((rows, half), f32),
            pltpu.VMEM((rows, half), f32),
            pltpu.VMEM((2 * depth, rows, half), f32),
            pltpu.VMEM((2, rows, half), f32),
            pltpu.VMEM((2, rows, LANES), f32),
            pltpu.VMEM((rows, half), f32),
            pltpu.VMEM((rows, half), f32),
            pltpu.VMEM((2, rows, half), f32),
            pltpu.VMEM((rows, half), jnp.int32),
            pltpu.VMEM((2, rows, half), f32),
            pltpu.VMEM((2, rows, half), f32),
            pltpu.VMEM((4, 2, 2, half), f32),
            pltpu.VMEM((4, 2, 2, 2, half), f32),
            pltpu.VMEM((3, 2, rows, LANES), f32),
            pltpu.VMEM((3, 2, 2, rows, LANES), f32),
            pltpu.VMEM((3, rows, half), f32),
            pltpu.VMEM((n_tile, 2 * slots), f32),
            pltpu.VMEM((n_tile, slots), f32),
            pltpu.VMEM((n_tile, slots), jnp.int32),
            pltpu.VMEM((1, n_tile), jnp.int32),
            pltpu.SemaphoreType.DMA((11,)),
            pltpu.SemaphoreType.DMA,
            pltpu.SemaphoreType.DMA((groups,)),
            pltpu.SemaphoreType.DMA((2,)),
            pltpu.SemaphoreType.DMA((2,)),
            pltpu.SemaphoreType.DMA((2,)),
            pltpu.SemaphoreType.DMA((4, 2, 2)),
            pltpu.SemaphoreType.DMA((4, 2, 2)),
            pltpu.SemaphoreType.DMA((3, 2)),
            pltpu.SemaphoreType.DMA((3, 2)),
            pltpu.SemaphoreType.DMA((3,)),
            pltpu.SemaphoreType.DMA((3,)),
            pltpu.SemaphoreType.DMA((2,)),
            pltpu.SemaphoreType.DMA((2,)),
            pltpu.SemaphoreType.DMA((2,)),
        ],
        compiler_params=pltpu.CompilerParams(
            collective_id=0, has_side_effects=True, vmem_limit_bytes=VMEM_BYTES
        ),
    )(
        velocity,
        friction,
        thickness,
        rate,
        driving,
        ice_mask,
        obs_velocity.reshape(n_tile, 2 * slots),
        obs_weight.reshape(n_tile, slots),
        obs_cells.reshape(n_tile, slots),
        obs_counts.reshape(1, n_tile),
    )
    return friction_out, velocity_out


def solution(mesh):
    placed = (
        P(None, "tile", None),
        P("tile", None),
        P("tile", None),
        P("layer", "tile", None),
        P(None, "tile", None),
        P("tile", None),
        P("tile", "layer", None, None),
        P("tile", "layer", None, None),
        P("tile", "layer", None, None),
        P("tile", "layer", None),
    )
    return jax.shard_map(
        body,
        mesh=mesh,
        in_specs=placed,
        out_specs=(P("tile", None), P(None, "tile", None)),
        check_vma=False,
    )
```

time: 52.5 us -> 48.2 us (0.918)
  Pallas kernels: 49.3 us -> 45.1 us
    pallas_call x1, Pallas kernels: 49.3 us -> 45.1 us  [body(): pl.pallas_call(functools.partial(kernel, sides, n_layer), out_shape=(jax....]
where the time goes in v3:
time: 48.2 us; the launch traced here: 48.1 us
  Pallas kernels  45.1 us (94%)
  local copies, waits for them, and re-layouts  2.42 us (5%)
  between operations  0.65 us (1%)
    pallas_call x1, Pallas kernels, body(): pl.pallas_call(functools.partial(kernel, sides, n_layer), out_shape=(jax....  45.1 us
    unnamed x4, local copies, waits for them, and re-layouts  2.42 us

profile of v3, /device:TPU:1, one launch (start us, length us, event | category | flops | bytes accessed | tf_op | source)
XLA Modules:
  0.0 48.1 jit_solution(1890608768364988497)
XLA Ops:
  0.6 45.1 %shard_map.113 = (f32[16,3072]{1,0:T(8,128)}, f32[2,16,3072]{2,1,0:T(8,128)}) custom-call(f32[2,16,3072]{2,1,0:T(8,128)} %velocity.1, f32[16,3072]{1,0:T(8,128)} %friction.1, f32[16,3072]{1,0:T(8,128)} %thickness.1, f32[4,16,3072]{2,1,0:T(8,128)} %rate.1, f32[2,16,3072]{2,1,0:T(8,128)} %driving.1, s32[16,3072]{1,0:T(8,128)} %ice_mask.1, f32[64,256]{1,0:T(8,128)} %bitcast.4, ...), custom_call_target="tpu_custom_call" | custom-call | tf_op jit(solution)/shard_map/pallas_call | solution.py:497
  45.7 0.0 copy-start
  45.7 1.7 %copy.14 = f32[16,3072]{1,0:T(8,128)} copy(f32[16,3072]{1,0:T(8,128)} %get-tuple-element.4) | data formatting | bytes 393216
  47.4 0.0 copy-done
  47.4 0.7 %copy.15 = f32[2,16,3072]{2,1,0:T(8,128)} copy(f32[2,16,3072]{2,1,0:T(8,128)S(1)} %copy-done) | data formatting | bytes 786432
Async XLA Ops:
  45.7 1.7 %copy-start = (f32[2,16,3072]{2,1,0:T(8,128)S(1)}, f32[2,16,3072]{2,1,0:T(8,128)}, u32[]{:S(2)}) copy-start(f32[2,16,3072]{2,1,0:T(8,128)} %get-tuple-element.5) | copy-start | bytes 1179652

commit v4 on v3

--- a/solution.py
+++ b/solution.py
@@ -45,7 +45,7 @@
     received,
     left_sides,
     right_sides,
-    total,
+    totals,
     fields,
     from_sibling,
     chip_sum,
@@ -65,7 +65,6 @@
     row_recv,
     col_send,
     col_recv,
-    result,
     seen_in,
     weight_in,
     cells_in,
@@ -84,7 +83,6 @@
     sum_recv_sems,
     out_send_sems,
     out_recv_sems,
-    own_sems,
 ):
     n_x, groups, n_y = sides
     per_group = n_x * n_y
@@ -98,6 +96,7 @@
     total_layers = depth * n_layer
     slots = obs_weight.shape[-1]
     marks = rows * n_layer
+    side_marks = CHANNELS * PIECES * marks // 2
     core = lax.rem(l, 2)
     chip = l // 2
     sibling = chip * 2 + (1 - core)
@@ -141,23 +140,26 @@
     barrier = pltpu.get_barrier_semaphore()
     x, z, y = t // (groups * n_y), lax.rem(t // n_y, groups), lax.rem(t, n_y)
 
-    def peer(turn):
-        ring = turn // per_group
-        step = lax.rem(ring, 2)
-        hop = step * ((ring + 1) // 2) + (1 - step) * (groups - ring // 2)
-        to_x = lax.rem(x + lax.rem(turn // n_y, n_x), n_x)
-        to_z = lax.rem(z + hop, groups)
-        to_y = lax.rem(y + turn, n_y)
-        return (to_x * groups + to_z) * n_y + to_y
+    along_x = [lax.rem(x + k, n_x) * (groups * n_y) for k in range(n_x)]
+    along_y = [lax.rem(y + k, n_y) for k in range(n_y)]
+
+    def ring_of(ring):
+        odd_ring = lax.rem(ring, 2)
+        hop = odd_ring * ((ring + 1) // 2) + (1 - odd_ring) * (groups - ring // 2)
+        to_z = lax.rem(z + hop, groups) * n_y
+        return [to_x + to_z + to_y for to_x in along_x for to_y in along_y]
 
     def greet_one(tile, layer):
         pl.semaphore_signal(barrier, inc=1, device_id=(tile, layer), device_id_type=MESH)
 
     def greet(turn, carry):
-        greet_one(peer(n_tile - turn), l)
+        for tile in ring_of(groups - turn):
+            greet_one(tile, l)
         return carry
 
-    lax.fori_loop(1, n_tile, greet, 0)
+    lax.fori_loop(1, groups, greet, 0)
+    for tile in ring_of(0)[1:]:
+        greet_one(tile, l)
     greet_one(above, partner)
     greet_one(below, partner)
     for layer in (partner, across, sibling):
@@ -235,19 +237,25 @@
     own_block = pltpu.make_async_copy(packed.at[t], received.at[0], obs_recv_sems.at[0])
     own_block.start()
 
-    def send_obs(turn, carry):
-        to = peer(turn)
+    def send_obs(tile, ring, k):
         remote(
-            packed.at[to],
-            received.at[turn],
+            packed.at[tile],
+            received.at[ring * per_group + k],
             obs_send_sem,
-            obs_recv_sems.at[turn // per_group],
-            to,
+            obs_recv_sems.at[ring],
+            tile,
             l,
         ).start()
+
+    def send_ring(ring, carry):
+        for k, tile in enumerate(ring_of(ring)):
+            send_obs(tile, ring, k)
         return carry
 
-    lax.fori_loop(1, n_tile, send_obs, 0)
+    for k, tile in enumerate(ring_of(0)):
+        if k > 0:
+            send_obs(tile, 0, k)
+    lax.fori_loop(1, groups, send_ring, 0)
     rate_copy = remote(
         rate.at[:, :, sibling_columns],
         rates.at[pl.ds(core * depth, depth)],
@@ -355,7 +363,8 @@
         wait(row_copies(0))
         send_part(0, *first_state())
 
-    total[...] = jnp.zeros_like(total)
+    for total in totals:
+        total[...] = jnp.zeros_like(total)
     mark_id = lax.broadcasted_iota(jnp.int32, (marks, slots), 0).astype(jnp.float32)
     lane_id = lax.broadcasted_iota(jnp.int32, (slots, quarter), 1).astype(jnp.float32)
 
@@ -377,48 +386,65 @@
         for b in range(per_group):
             hit = mark[b : b + 1, :] == mark_id
             for p, piece in enumerate(pieces):
-                left_side[p * marks : (p + 1) * marks, b * slots : (b + 1) * slots] = jnp.where(
-                    hit, piece[b : b + 1, :], 0.0
-                ).astype(jnp.bfloat16)
+                marked = jnp.where(hit, piece[b : b + 1, :], 0.0).astype(jnp.bfloat16)
+                for side in range(2):
+                    at = side * side_marks + p * (marks // 2)
+                    left_side[at : at + marks // 2, b * slots : (b + 1) * slots] = marked[
+                        side * (marks // 2) : (side + 1) * (marks // 2)
+                    ]
             right_side[b * slots : (b + 1) * slots, :] = jnp.where(
                 column[:, b : b + 1] == lane_id, 1.0, 0.0
             ).astype(jnp.bfloat16)
 
-    def multiply(left_side, right_side):
+    def multiply(left_side, right_side, total):
         total[...] += jnp.dot(left_side[...], right_side[...], preferred_element_type=jnp.float32)
 
-    even, odd = (left_sides[0], right_sides[0]), (left_sides[1], right_sides[1])
-    turns = groups // 2
+    def multiply_side(side, left_side, right_side, total):
+        part = pl.ds(pl.multiple_of(side * side_marks, side_marks), side_marks)
+        total[part, :] += jnp.dot(
+            left_side[part, :], right_side[...], preferred_element_type=jnp.float32
+        )
+
+    even = (left_sides[0], right_sides[0], totals[0])
+    odd = (left_sides[1], right_sides[1], totals[1])
+    turns = groups // 2 - 1
 
     def two_groups(turn, carry):
         arrive(2 * turn + 1)
-        pl.when(turn < turns - 1)(lambda: arrive(2 * turn + 2))
+        arrive(2 * turn + 2)
         pl.when(turn == min(IT1_AT, turns - 1))(first_part)
-        build(2 * turn + 1, *odd)
+        build(2 * turn + 1, *odd[:2])
         multiply(*even)
-        build(lax.rem(2 * turn + 2, groups), *even)
+        build(2 * turn + 2, *even[:2])
         multiply(*odd)
         return carry
-
-    arrive(0)
-    build(0, *even)
-    lax.fori_loop(0, turns, two_groups, 0)
 
     def collect(side):
         for channel in range(CHANNELS):
             for q in range(2):
                 field = None
                 for piece in range(PIECES):
-                    at = (channel * PIECES + piece) * marks + (side * 2 + q) * rows
-                    part = total[pl.ds(pl.multiple_of(at, rows), rows), :]
-                    field = part if field is None else field + part
+                    at = side * side_marks + ((channel * PIECES + piece) * 2 + q) * rows
+                    part = pl.ds(pl.multiple_of(at, rows), rows)
+                    value = totals[0][part, :] + totals[1][part, :]
+                    field = value if field is None else field + value
                 fields[side, channel, :, q * quarter : (q + 1) * quarter] = field
 
+    arrive(0)
+    build(0, *even[:2])
+    lax.fori_loop(0, turns, two_groups, 0)
+    arrive(groups - 1)
+    build(groups - 1, *odd[:2])
+
+    multiply_side(1 - core, *even)
+    multiply_side(1 - core, *odd)
     collect(1 - core)
     sum_copy = remote(
         fields.at[1 - core], from_sibling, sum_send_sems.at[0], sum_recv_sems.at[0], t, sibling
     )
     sum_copy.start()
+    multiply_side(core, *even)
+    multiply_side(core, *odd)
     collect(core)
 
     strain, speed, fric = first_state()
@@ -451,20 +477,19 @@
     fric = drag(coeff)
     send_part(1, strain, speed, fric)
     speed = new_speed(1, strain, speed, fric)
-    result[0] = speed[0]
-    result[1] = speed[1]
+    velocity_out[0, :, columns] = speed[0]
+    velocity_out[1, :, columns] = speed[1]
+    finals = [
+        remote(out, out, out_send_sems.at[k], out_recv_sems.at[k], t, sibling)
+        for k, out in enumerate(
+            (velocity_out.at[:, :, columns], friction_out.at[:, columns])
+        )
+    ]
+    finals[0].start()
     chip_copy.wait()
     sums = [chip_sum[k] + other_sum[k] for k in range(CHANNELS)]
-    result[2] = coeff - 0.2 * fric * misfit(sums, speed)
-
-    finals = []
-    for k, dst in ((0, velocity_out.at[:, :, columns]), (1, friction_out.at[:, columns])):
-        src = result.at[0:2] if k == 0 else result.at[2]
-        finals.append(
-            remote(src, dst, out_send_sems.at[k], out_recv_sems.at[k], t, sibling)
-        )
-        finals.append(pltpu.make_async_copy(src, dst, own_sems.at[k]))
-    start(finals)
+    friction_out[:, columns] = coeff - 0.2 * fric * misfit(sums, speed)
+    finals[1].start()
     wait(finals)
 
     blocks = packed.at[pl.ds(1, n_tile - 1)]
@@ -488,7 +513,7 @@
     half, quarter = width // 2, width // n_layer
     slots = obs_weight.shape[-1]
     depth = rate.shape[0]
-    sides = (4, n_tile // 8, 2) if n_tile % 8 == 0 else (1, n_tile // 2, 2)
+    sides = (4, n_tile // 8, 2) if n_tile % 8 == 0 else (1, n_tile, 1)
     marks = rows * n_layer
     groups = sides[1]
     chunk = (n_tile // groups) * slots
@@ -497,17 +522,17 @@
     friction_out, velocity_out = pl.pallas_call(
         functools.partial(kernel, sides, n_layer),
         out_shape=(
-            jax.ShapeDtypeStruct(friction.shape, f32),
-            jax.ShapeDtypeStruct(velocity.shape, f32),
+            pltpu.VMEM(friction.shape, f32),
+            pltpu.VMEM(velocity.shape, f32),
         ),
         in_specs=[in_hbm] * 10,
-        out_specs=(in_hbm, in_hbm),
+        out_specs=[pl.BlockSpec(memory_space=pltpu.VMEM)] * 2,
         scratch_shapes=[
             pltpu.VMEM((n_tile, 4, slots), f32),
             pltpu.VMEM((n_tile, 4, slots), f32),
             [pltpu.VMEM((CHANNELS * PIECES * marks, chunk), jnp.bfloat16)] * 2,
             [pltpu.VMEM((chunk, quarter), jnp.bfloat16)] * 2,
-            pltpu.VMEM((CHANNELS * PIECES * marks, quarter), f32),
+            [pltpu.VMEM((CHANNELS * PIECES * marks, quarter), f32)] * 2,
             pltpu.VMEM((2, CHANNELS, rows, half), f32),
             pltpu.VMEM((CHANNELS, rows, half), f32),
             pltpu.VMEM((CHANNELS, rows, half), f32),
@@ -527,7 +552,6 @@
             pltpu.VMEM((4, 2, 2, 2, half), f32),
             pltpu.VMEM((3, 2, rows, LANES), f32),
             pltpu.VMEM((3, 2, 2, rows, LANES), f32),
-            pltpu.VMEM((3, rows, half), f32),
             pltpu.VMEM((n_tile, 2 * slots), f32),
             pltpu.VMEM((n_tile, slots), f32),
             pltpu.VMEM((n_tile, slots), jnp.int32),
@@ -544,7 +568,6 @@
             pltpu.SemaphoreType.DMA((3, 2)),
             pltpu.SemaphoreType.DMA((3,)),
             pltpu.SemaphoreType.DMA((3,)),
-            pltpu.SemaphoreType.DMA((2,)),
             pltpu.SemaphoreType.DMA((2,)),
             pltpu.SemaphoreType.DMA((2,)),
         ],

time: 48.2 us -> 46 us (0.954)
  Pallas kernels: 45.1 us -> 43.8 us
  local copies, waits for them, and re-layouts: 2.42 us -> 1.42 us
    pallas_call x1, Pallas kernels: 45.1 us -> 43.8 us  [body(): pl.pallas_call(functools.partial(kernel, sides, n_layer), out_shape=(pltp...]
    unnamed x4 -> x2, local copies, waits for them, and re-layouts: 2.42 us -> 1.42 us
where the time goes in v4:
time: 46 us; the launch traced here: 45.9 us
  Pallas kernels  43.8 us (95%)
  local copies, waits for them, and re-layouts  1.42 us (3%)
  between operations  0.64 us (1%)
    pallas_call x1, Pallas kernels, body(): pl.pallas_call(functools.partial(kernel, sides, n_layer), out_shape=(pltp...  43.8 us
    unnamed x2, local copies, waits for them, and re-layouts  1.42 us

profile of v4, /device:TPU:1, one launch (start us, length us, event | category | flops | bytes accessed | tf_op | source)
XLA Modules:
  0.0 45.9 jit_solution(1144582059105392352)
XLA Ops:
  0.6 43.8 %shard_map.113 = (f32[16,3072]{1,0:T(8,128)S(1)}, f32[2,16,3072]{2,1,0:T(8,128)S(1)}) custom-call(f32[2,16,3072]{2,1,0:T(8,128)} %velocity.1, f32[16,3072]{1,0:T(8,128)} %friction.1, f32[16,3072]{1,0:T(8,128)} %thickness.1, f32[4,16,3072]{2,1,0:T(8,128)} %rate.1, f32[2,16,3072]{2,1,0:T(8,128)} %driving.1, s32[16,3072]{1,0:T(8,128)} %ice_mask.1, ...), custom_call_target="tpu_custom_call" | custom-call | tf_op jit(solution)/shard_map/pallas_call | solution.py:522
  44.4 0.7 %copy.14 = f32[16,3072]{1,0:T(8,128)} copy(f32[16,3072]{1,0:T(8,128)S(1)} %get-tuple-element.2) | data formatting | bytes 393216
  45.1 0.7 %copy.15 = f32[2,16,3072]{2,1,0:T(8,128)} copy(f32[2,16,3072]{2,1,0:T(8,128)S(1)} %get-tuple-element.3) | data formatting | bytes 786432

commit v5 on v4

--- a/solution.py
+++ b/solution.py
@@ -12,7 +12,6 @@
 LANES = 128
 PIECES = 3
 VMEM_BYTES = 58 * 1024 * 1024
-IT1_AT = 1
 
 CHANNELS = 3
 
@@ -134,9 +133,6 @@
             rate.at[:, :, columns], rates.at[pl.ds(core * depth, depth)], load_sems.at[10]
         ),
     ]
-    for load in loads:
-        load.start()
-
     barrier = pltpu.get_barrier_semaphore()
     x, z, y = t // (groups * n_y), lax.rem(t // n_y, groups), lax.rem(t, n_y)
 
@@ -164,6 +160,9 @@
     greet_one(below, partner)
     for layer in (partner, across, sibling):
         greet_one(t, layer)
+
+    for load in loads:
+        load.start()
 
     for load in loads[:4]:
         load.wait()
@@ -317,7 +316,7 @@
     chip_layers = 2 * depth
     first_layer = (chip * chip_layers).astype(jnp.float32)
 
-    def send_part(turn, strain, speed, fric):
+    def make_part(turn, strain, speed, fric):
         exx, eyy, exy = strain
         e2 = exx * exx + eyy * eyy + exx * eyy + exy * exy + 0.05
         b2 = 0.25 * fric * fric * (speed[0] * speed[0] + speed[1] * speed[1])
@@ -332,6 +331,9 @@
         sxx, syy, sxy = stresses(strain, part)
         phase = 2 * turn + 1
         stage(phase, (sxx, sxy), (sxy, syy))
+
+    def send_part(turn):
+        phase = 2 * turn + 1
         start(row_copies(phase))
         part_copy(turn).start()
         start(col_copies(phase))
@@ -356,12 +358,6 @@
     def first_state():
         speed = (vel[0], vel[1])
         return strains(speed, 0, (edge[0], edge[1])), speed, drag(fric_in[...])
-
-    def first_part():
-        wait(loads[6:])
-        rate_copy.wait()
-        wait(row_copies(0))
-        send_part(0, *first_state())
 
     for total in totals:
         total[...] = jnp.zeros_like(total)
@@ -412,7 +408,6 @@
     def two_groups(turn, carry):
         arrive(2 * turn + 1)
         arrive(2 * turn + 2)
-        pl.when(turn == min(IT1_AT, turns - 1))(first_part)
         build(2 * turn + 1, *odd[:2])
         multiply(*even)
         build(2 * turn + 2, *even[:2])
@@ -432,7 +427,21 @@
 
     arrive(0)
     build(0, *even[:2])
-    lax.fori_loop(0, turns, two_groups, 0)
+
+    arrive(1)
+    arrive(2)
+    wait(loads[6:])
+    rate_copy.wait()
+    wait(row_copies(0))
+    build(1, *odd[:2])
+    strain, speed, fric = first_state()
+    make_part(0, strain, speed, fric)
+    multiply(*even)
+    build(2, *even[:2])
+    multiply(*odd)
+    send_part(0)
+
+    lax.fori_loop(1, turns, two_groups, 0)
     arrive(groups - 1)
     build(groups - 1, *odd[:2])
 
@@ -443,13 +452,13 @@
         fields.at[1 - core], from_sibling, sum_send_sems.at[0], sum_recv_sems.at[0], t, sibling
     )
     sum_copy.start()
+
+    strain, speed, fric = first_state()
+    speed = new_speed(0, strain, speed, fric)
+    stage(2, speed, speed)
     multiply_side(core, *even)
     multiply_side(core, *odd)
     collect(core)
-
-    strain, speed, fric = first_state()
-    speed = new_speed(0, strain, speed, fric)
-    stage(2, speed, speed)
     swaps = row_copies(2) + col_copies(2)
     start(swaps)
 
@@ -475,7 +484,8 @@
     coeff = fric_in[...] - 0.2 * fric * (along_send[...] + along_recv[...])
 
     fric = drag(coeff)
-    send_part(1, strain, speed, fric)
+    make_part(1, strain, speed, fric)
+    send_part(1)
     speed = new_speed(1, strain, speed, fric)
     velocity_out[0, :, columns] = speed[0]
     velocity_out[1, :, columns] = speed[1]

time: 46 us -> 45.9 us (level)
  no operation moved by 1% of the time
where the time goes in v5:
time: 45.9 us; the launch traced here: 45.8 us
  Pallas kernels  43.7 us (95%)
  local copies, waits for them, and re-layouts  1.42 us (3%)
  between operations  0.64 us (1%)
    pallas_call x1, Pallas kernels, body(): pl.pallas_call(functools.partial(kernel, sides, n_layer), out_shape=(pltp...  43.7 us
    unnamed x2, local copies, waits for them, and re-layouts  1.42 us

profile of v5, /device:TPU:1, one launch (start us, length us, event | category | flops | bytes accessed | tf_op | source)
XLA Modules:
  0.0 45.8 jit_solution(9302439848126672453)
XLA Ops:
  0.6 43.7 %shard_map.113 = (f32[16,3072]{1,0:T(8,128)S(1)}, f32[2,16,3072]{2,1,0:T(8,128)S(1)}) custom-call(f32[2,16,3072]{2,1,0:T(8,128)} %velocity.1, f32[16,3072]{1,0:T(8,128)} %friction.1, f32[16,3072]{1,0:T(8,128)} %thickness.1, f32[4,16,3072]{2,1,0:T(8,128)} %rate.1, f32[2,16,3072]{2,1,0:T(8,128)} %driving.1, s32[16,3072]{1,0:T(8,128)} %ice_mask.1, ...), custom_call_target="tpu_custom_call" | custom-call | tf_op jit(solution)/shard_map/pallas_call | solution.py:532
  44.4 0.7 %copy.14 = f32[16,3072]{1,0:T(8,128)} copy(f32[16,3072]{1,0:T(8,128)S(1)} %get-tuple-element.2) | data formatting | bytes 393216
  45.0 0.7 %copy.15 = f32[2,16,3072]{2,1,0:T(8,128)} copy(f32[2,16,3072]{2,1,0:T(8,128)S(1)} %get-tuple-element.3) | data formatting | bytes 786432

commit v6 on v5

--- a/solution.py
+++ b/solution.py
@@ -429,7 +429,6 @@
     build(0, *even[:2])
 
     arrive(1)
-    arrive(2)
     wait(loads[6:])
     rate_copy.wait()
     wait(row_copies(0))
@@ -437,6 +436,7 @@
     strain, speed, fric = first_state()
     make_part(0, strain, speed, fric)
     multiply(*even)
+    arrive(2)
     build(2, *even[:2])
     multiply(*odd)
     send_part(0)

time: 45.9 us -> 46.5 us (1.013)
  Pallas kernels: 43.7 us -> 44.4 us
    pallas_call x1, Pallas kernels: 43.7 us -> 44.4 us  [body(): pl.pallas_call(functools.partial(kernel, sides, n_layer), out_shape=(pltp...]
where the time goes in v6:
time: 46.5 us; the launch traced here: 46.4 us
  Pallas kernels  44.4 us (95%)
  local copies, waits for them, and re-layouts  1.42 us (3%)
  between operations  0.64 us (1%)
    pallas_call x1, Pallas kernels, body(): pl.pallas_call(functools.partial(kernel, sides, n_layer), out_shape=(pltp...  44.4 us
    unnamed x2, local copies, waits for them, and re-layouts  1.42 us

profile of v6, /device:TPU:1, one launch (start us, length us, event | category | flops | bytes accessed | tf_op | source)
XLA Modules:
  0.0 46.4 jit_solution(2856742736125142347)
XLA Ops:
  0.6 44.4 %shard_map.113 = (f32[16,3072]{1,0:T(8,128)S(1)}, f32[2,16,3072]{2,1,0:T(8,128)S(1)}) custom-call(f32[2,16,3072]{2,1,0:T(8,128)} %velocity.1, f32[16,3072]{1,0:T(8,128)} %friction.1, f32[16,3072]{1,0:T(8,128)} %thickness.1, f32[4,16,3072]{2,1,0:T(8,128)} %rate.1, f32[2,16,3072]{2,1,0:T(8,128)} %driving.1, s32[16,3072]{1,0:T(8,128)} %ice_mask.1, ...), custom_call_target="tpu_custom_call" | custom-call | tf_op jit(solution)/shard_map/pallas_call | solution.py:532
  45.0 0.7 %copy.14 = f32[16,3072]{1,0:T(8,128)} copy(f32[16,3072]{1,0:T(8,128)S(1)} %get-tuple-element.2) | data formatting | bytes 393216
  45.7 0.7 %copy.15 = f32[2,16,3072]{2,1,0:T(8,128)} copy(f32[2,16,3072]{2,1,0:T(8,128)S(1)} %get-tuple-element.3) | data formatting | bytes 786432
